TPU v7x, 32 devices: a whole 2x2x4 slice. The times are simulated.
32 devices in a mesh: ctx: 8 (over y, x, core), head: 4 (over z).
Axes of the slice: x: 2, y: 2, z: 4, core: 2. Of those that a mesh axis runs over, the one named last changes fastest.
Arguments:
- queries: bfloat16 [16384, 4096], P('ctx', 'head'), may hold values from -2 to 2
- key_rows: bfloat16 [16384, 4096], P('ctx', 'head'), may hold values from -2 to 2
- value_rows: bfloat16 [16384, 4096], P('ctx', 'head'), may hold values from -6 to 6
- log_decay: bfloat16 [16384, 32], P('ctx', 'head'), may hold values from -0.4 to 0, as said below
- norm_gain: float32 [4096], P('head'), may hold values from 0.1 to 1.9
- doc_lengths: int32 [16], replicated, may hold values from 1 to 8192, 16384 in all
- packing: int32 [128], replicated, may hold values from 0 to 127, as said below
Outputs:
- mixed: bfloat16 [16384, 4096], P('ctx', 'head')
Inputs may be any that keep to these rules, and one draw needn't show every extreme that they name: packing is a permutation of the blocks. Loader block b is block b % 16 of ctx device b // 16; packed block p belongs to owner p // 16. Of the blocks of one loader, each owner receives none or exactly 4. `doc_lengths`: the lengths sum to 16384; the longest is 8192. `log_decay`: negative logarithms of decays.
All inputs are finite; a program needn't handle non-finite values.
Results may differ from a plain program's by a relative error of at most 0.0055.
Values may be sent and summed in bfloat16 or wider, within the bound.
A program may use at most 192 MiB of HBM per device.

v0:
```python
import jax
import jax.numpy as jnp
from jax import lax
from jax.sharding import PartitionSpec as P

BLOCK = 128


def from_behind(x, axis, by):
    count = lax.axis_size(axis)
    pairs = [(i, i + by) for i in range(count) if 0 <= i + by < count]
    return lax.ppermute(x, axis, pairs)


def state_pass(key_blocks, value_blocks, decay_blocks, first, docid):
    block_log = jnp.cumsum(decay_blocks.astype(jnp.float32), axis=1)
    block_total = block_log[:, -1, :]
    seen = jnp.cumsum(first, axis=1)
    reach_block = (seen == 0).astype(jnp.float32)
    unbroken = (seen[:, -1] == 0).astype(jnp.float32)
    same_last = (docid == docid[:, -1:]).astype(jnp.float32)
    keep = jnp.exp(block_total[:, None, :] - block_log) * same_last[:, :, None]
    key_decayed = (key_blocks.astype(jnp.float32) * keep[..., None]).astype(jnp.bfloat16)
    own = jnp.einsum(
        "nshd,nshe->nhde", key_decayed, value_blocks, preferred_element_type=jnp.float32
    )
    gate = jnp.exp(block_total) * unbroken[:, None]

    def advance(state, item):
        factor, term = item
        return (factor[:, None, None] * state + term, state)

    start = jnp.zeros(own.shape[1:], jnp.float32)
    s_end, states = lax.scan(advance, start, (gate, own))
    prior = jnp.cumsum(block_total, axis=0) - block_total
    segment_log = block_log + prior[:, None, :]
    block_starts = seen[:, -1]
    before = jnp.cumsum(block_starts) - block_starts
    reach_segment = (seen + before[:, None] == 0).astype(jnp.float32)
    clean = (jnp.sum(first) == 0).astype(jnp.float32)
    decay_all = jnp.exp(segment_log[-1, -1]) * clean
    return (block_log, reach_block, states, segment_log, reach_segment, decay_all, s_end)


def query_pass(query_blocks, key_blocks, value_blocks, block_log, reach_block, states, docid):
    length = docid.shape[1]
    order = jnp.arange(length)
    causal = order[:, None] >= order[None, :]
    allowed = causal[None] & (docid[:, :, None] == docid[:, None, :])
    by_head = jnp.transpose(block_log, (0, 2, 1))
    gaps = by_head[:, :, :, None] - by_head[:, :, None, :]
    weight = jnp.where(allowed[:, None], jnp.exp(jnp.minimum(gaps, 0.0)), 0.0)
    scores = jnp.einsum(
        "nthd,nshd->nhts", query_blocks, key_blocks, preferred_element_type=jnp.float32
    )
    weights = (scores * weight).astype(jnp.bfloat16)
    intra = jnp.einsum("nhts,nshd->nthd", weights, value_blocks, preferred_element_type=jnp.float32)
    query_decayed = (
        query_blocks.astype(jnp.float32) * (jnp.exp(block_log) * reach_block[:, :, None])[..., None]
    ).astype(jnp.bfloat16)
    inter = jnp.einsum(
        "nthd,nhde->nthe",
        query_decayed,
        states.astype(jnp.bfloat16),
        preferred_element_type=jnp.float32,
    )
    return intra + inter


def carry_in(decay_all, s_end, devices):
    zero_state = jnp.zeros(s_end.shape, jnp.float32)

    def forward(index, pair):
        arrived = from_behind(pair[1], "ctx", 1)
        return (arrived, decay_all[:, None, None] * arrived + s_end)

    arrival, leaving = lax.fori_loop(0, devices - 1, forward, (zero_state, s_end))
    return arrival


def body(queries, key_rows, value_rows, log_decay, norm_gain, doc_lengths, packing):
    rows, width = queries.shape
    heads = log_decay.shape[1]
    head_size = width // heads
    blocks = rows // BLOCK
    devices = lax.axis_size("ctx")
    mine = lax.axis_index("ctx")
    total_blocks = packing.shape[0]
    capacity = (2 * blocks + devices - 1) // devices
    owners = (packing // blocks).reshape(devices, blocks)
    local = jnp.arange(blocks, dtype=jnp.int32)
    earlier_mask = local[:, None] < local[None, :]
    same_owner = owners[:, :, None] == owners[:, None, :]
    ranks = jnp.sum((same_owner & earlier_mask[None]).astype(jnp.int32), axis=1)
    my_owner = lax.dynamic_index_in_dim(owners, mine, 0, keepdims=False)
    my_rank = lax.dynamic_index_in_dim(ranks, mine, 0, keepdims=False)
    slot_of = my_owner * capacity + my_rank
    slot_ids = jnp.arange(devices * capacity, dtype=jnp.int32)
    matched = slot_of[None, :] == slot_ids[:, None]
    source = jnp.sum(matched.astype(jnp.int32) * local[None, :], axis=1)
    filled = jnp.any(matched, axis=1)

    def outgoing(values):
        columns = values.shape[1]
        picked = jnp.take(values.reshape(blocks, BLOCK, columns), source, axis=0)
        kept = jnp.where(filled[:, None, None], picked, jnp.zeros((), values.dtype))
        return kept.reshape(devices, capacity * BLOCK, columns)

    target = mine * blocks + local
    block_index = jnp.arange(total_blocks, dtype=jnp.int32)
    wanted = packing[None, :] == target[:, None]
    loader_block = jnp.sum(wanted.astype(jnp.int32) * block_index[None, :], axis=1)
    column = loader_block // blocks * capacity + jnp.take(ranks.reshape(-1), loader_block)

    def arriving(values):
        return jnp.take(values.reshape(devices * capacity, BLOCK, values.shape[2]), column, axis=0)

    starts = jnp.cumsum(doc_lengths) - doc_lengths
    positions = mine * rows + jnp.arange(rows, dtype=jnp.int32)
    first = (
        jnp.any(positions[:, None] == starts[None, :], axis=1)
        .astype(jnp.int32)
        .reshape(blocks, BLOCK)
    )
    docid = (
        jnp.sum((starts[None, :] <= positions[:, None]).astype(jnp.int32), axis=1) - 1
    ).reshape(blocks, BLOCK)
    got_queries, got_keys, got_values, received_decay = (
        lax.all_to_all(outgoing(queries), "ctx", split_axis=0, concat_axis=0, tiled=True),
        lax.all_to_all(outgoing(key_rows), "ctx", split_axis=0, concat_axis=0, tiled=True),
        lax.all_to_all(outgoing(value_rows), "ctx", split_axis=0, concat_axis=0, tiled=True),
        lax.all_to_all(outgoing(log_decay), "ctx", split_axis=0, concat_axis=0, tiled=True),
    )
    key_blocks = arriving(got_keys).reshape(blocks, BLOCK, heads, head_size)
    value_blocks = arriving(got_values).reshape(blocks, BLOCK, heads, head_size)
    decay_blocks = arriving(received_decay)
    block_log, reach_block, states, segment_log, reach_segment, decay_all, s_end = state_pass(
        key_blocks, value_blocks, decay_blocks, first, docid
    )
    arrival = carry_in(decay_all, s_end, devices)
    query_blocks = arriving(got_queries).reshape(blocks, BLOCK, heads, head_size)
    local_out = query_pass(
        query_blocks, key_blocks, value_blocks, block_log, reach_block, states, docid
    )
    scaled = (
        query_blocks.astype(jnp.float32)
        * (jnp.exp(segment_log) * reach_segment[:, :, None])[..., None]
    ).astype(jnp.bfloat16)
    carried = jnp.einsum(
        "nthd,hde->nthe", scaled, arrival.astype(jnp.bfloat16), preferred_element_type=jnp.float32
    )
    total = (local_out + carried).reshape(rows, width)
    squares = lax.psum(jnp.sum(total * total, axis=1), "head")
    columns_all = width * lax.axis_size("head")
    scale = lax.rsqrt(squares / columns_all + 1e-05)
    return (total * scale[:, None] * norm_gain[None, :]).astype(jnp.bfloat16)


def solution(mesh):
    placed = (
        P("ctx", "head"),
        P("ctx", "head"),
        P("ctx", "head"),
        P("ctx", "head"),
        P("head"),
        P(),
        P(),
    )
    return jax.shard_map(
        body, mesh=mesh, in_specs=placed, out_specs=P("ctx", "head"), check_vma=False
    )
```

profile of v0, /device:TPU:4, one launch (start us, length us, event | category | flops | bytes accessed | tf_op | source)
XLA Modules:
  0.0 560.9 jit_solution(11043720025341162474)
XLA Ops:
  2.8 4.2 all-to-all-start.3
  7.1 7.1 %gather_fusion.7 = bf16[32,128,1024]{2,1,0:T(8,128)(2,1)} fusion(bf16[16,128,1024]{2,1,0:T(8,128)(2,1)} %bitcast.99, s32[1024]{0:T(1024)S(1)} %pad_clamp_fusion.3), kind=kCustom, calls=%fused_computation.3.clone | custom fusion | bytes 16777344 | tf_op jit(solution)/shard_map/jit(_take)/gather | solution.py:105
  14.2 7.1 %gather_fusion.5 = bf16[32,128,1024]{2,1,0:T(8,128)(2,1)} fusion(bf16[16,128,1024]{2,1,0:T(8,128)(2,1)} %bitcast.100, s32[1024]{0:T(1024)S(1)} %pad_clamp_fusion.3), kind=kCustom, calls=%fused_computation.2.clone | custom fusion | bytes 16777344 | tf_op jit(solution)/shard_map/jit(_take)/gather | solution.py:105
  21.3 7.1 %gather_fusion.3 = bf16[32,128,1024]{2,1,0:T(8,128)(2,1)} fusion(bf16[16,128,1024]{2,1,0:T(8,128)(2,1)} %bitcast.101, s32[1024]{0:T(1024)S(1)} %pad_clamp_fusion.3), kind=kCustom, calls=%fused_computation.clone | custom fusion | bytes 16777344 | tf_op jit(solution)/shard_map/jit(_take)/gather | solution.py:105
  28.4 16.5 %select_select_fusion = (bf16[32,128,1024]{2,1,0:T(8,128)(2,1)}, bf16[32,128,1024]{2,1,0:T(8,128)(2,1)}, bf16[32,128,1024]{2,1,0:T(8,128)(2,1)}) fusion(bf16[32,128,1024]{2,1,0:T(8,128)(2,1)} %gather_fusion.7, pred[32]{0:T(512)(128)(4,1)S(1)} %compare_and_fusion.3, pred[32]{0:T(512)(128)(4,1)S(1)} %fusion.29, bf16[32,128,1024]{2,1,0:T(8,128)(2,1)} %gather_fusion.5, ...), kind=kLoop, calls=%fused_computation.22 | loop fusion | flops 25165824 | bytes 50331712 | tf_op jit(solution)/shard_map/jit(_where)/select_n | solution.py:106
  44.9 98.8 %all_to_all.20 = bf16[8,512,1024]{2,1,0:T(8,128)(2,1)} all-to-all(bf16[8,512,1024]{2,1,0:T(8,128)(2,1)} %bitcast.95), channel_id=1, replica_groups=mesh['ctx'=8,'head'=4] {'ctx'}, dimensions={0} | all-to-all | bytes 16777216 | tf_op jit(solution)/shard_map/all_to_all | solution.py:130
  143.8 97.5 %all_to_all.21 = bf16[8,512,1024]{2,1,0:T(8,128)(2,1)} all-to-all(bf16[8,512,1024]{2,1,0:T(8,128)(2,1)S(1)} %bitcast.94), channel_id=1, replica_groups=mesh['ctx'=8,'head'=4] {'ctx'}, dimensions={0} | all-to-all | bytes 16777216 | tf_op jit(solution)/shard_map/all_to_all | solution.py:129
  241.2 6.5 %all-to-all-start = ((bf16[8,512,1024]{2,1,0:T(8,128)(2,1)}), bf16[8,512,1024]{2,1,0:T(8,128)(2,1)}, u32[]{:S(2)}, u32[]{:S(2)}) async-start(bf16[8,512,1024]{2,1,0:T(8,128)(2,1)} %bitcast.91), calls=%async_computation | async-start | bytes 16777216 | tf_op jit(solution)/shard_map/all_to_all | solution.py:131
  253.8 23.3 %fusion.39 = f32[16,128,8]{2,0,1:T(8,128)S(1)} fusion(f32[16,128,8]{2,0,1:T(8,128)S(1)} %copy.160), kind=kOutput, calls=%fused_computation.123 | output fusion | flops 2080768 | bytes 131072 | tf_op jit(solution)/shard_map/jit(cumsum)/reduce_window_sum | solution.py:16
  277.4 2.1 exponential_multiply_fusion
  279.5 1.6 copy.178
  281.2 1.6 copy.167
  284.3 6.2 %gather_fusion.8 = bf16[16,128,1024]{2,1,0:T(8,128)(2,1)} fusion(bf16[32,128,1024]{2,1,0:T(8,128)(2,1)} %bitcast.97, s32[1024]{0:T(1024)S(1)} %pad_clamp_fusion.2), kind=kCustom, calls=%fused_computation.5.clone | custom fusion | bytes 8388672 | tf_op jit(solution)/shard_map/jit(_take)/gather | solution.py:116
  290.5 6.2 %gather_fusion.6 = bf16[16,128,1024]{2,1,0:T(8,128)(2,1)} fusion(bf16[32,128,1024]{2,1,0:T(8,128)(2,1)} %bitcast.98, s32[1024]{0:T(1024)S(1)} %pad_clamp_fusion.2), kind=kCustom, calls=%fused_computation.4.clone | custom fusion | bytes 8388672 | tf_op jit(solution)/shard_map/jit(_take)/gather | solution.py:116
  296.7 43.7 %all-to-all-done = bf16[8,512,1024]{2,1,0:T(8,128)(2,1)} async-done(((bf16[8,512,1024]{2,1,0:T(8,128)(2,1)}), bf16[8,512,1024]{2,1,0:T(8,128)(2,1)}, u32[]{:S(2)}, u32[]{:S(2)}) %all-to-all-start) | async-done | bytes 8388640 | tf_op jit(solution)/shard_map/all_to_all | solution.py:131
  340.4 6.2 %gather_fusion.4 = bf16[16,128,1024]{2,1,0:T(8,128)(2,1)} fusion(bf16[32,128,1024]{2,1,0:T(8,128)(2,1)} %bitcast.4, s32[1024]{0:T(1024)S(1)} %pad_clamp_fusion.2), kind=kCustom, calls=%fused_computation.1.clone | custom fusion | bytes 8388672 | tf_op jit(solution)/shard_map/jit(_take)/gather | solution.py:116
  346.5 8.9 %broadcast_select_fusion = (bf16[16,128,1024]{2,1,0:T(8,128)(2,1)}, bf16[16,128,1024]{2,1,0:T(8,128)(2,1)}, bf16[16,128,1024]{2,1,0:T(8,128)(2,1)}) fusion(bf16[16,128,1024]{2,1,0:T(8,128)(2,1)} %gather_fusion.8, pred[16]{0:T(512)(128)(4,1)S(1)} %get-tuple-element.129, bf16[16,128,1024]{2,1,0:T(8,128)(2,1)} %gather_fusion.6, ...), kind=kLoop, calls=%fused_computation.39 | loop fusion | flops 6291456 | bytes 25165840 | tf_op jit(solution)/shard_map/jit(_take)/select_n | solution.py:116
  355.5 6.4 %copy.150 = bf16[16,128,1024]{1,2,0:T(8,128)(2,1)} copy(bf16[16,128,1024]{2,1,0:T(8,128)(2,1)} %get-tuple-element.141) | data formatting | bytes 8388608 | tf_op jit(solution)/shard_map/jit(_take)/select_n | solution.py:116
  361.9 6.4 %copy.149 = bf16[16,128,1024]{1,2,0:T(8,128)(2,1)} copy(bf16[16,128,1024]{2,1,0:T(8,128)(2,1)} %get-tuple-element.142) | data formatting | bytes 8388608 | tf_op jit(solution)/shard_map/jit(_take)/select_n | solution.py:116
  368.2 6.4 %copy.192 = bf16[16,128,1024]{1,2,0:T(8,128)(2,1)} copy(bf16[16,128,1024]{2,1,0:T(8,128)(2,1)} %get-tuple-element.140) | data formatting | bytes 8388608 | tf_op jit(solution)/shard_map/reshape | solution.py:134
  374.6 9.7 %fusion.6 = f32[16,8,128,128]{3,2,1,0:T(8,128)} fusion(bf16[16,128,8,128]{1,3,2,0:T(8,128)(2,1)} %bitcast.102, bf16[16,128,8,128]{1,3,2,0:T(8,128)(2,1)} %bitcast.104, f32[16,128,8]{1,2,0:T(8,128)S(1)} %copy.167), kind=kOutput, calls=%fused_computation.29 | convolution fusion | flops 543162368 | bytes 16842752 | tf_op jit(solution)/shard_map/nshd,nshe->nhde/dot_general | solution.py:24
  384.3 31.0 %while.28 = (s32[]{:T(128)}, f32[8,128,128]{2,1,0:T(8,128)S(1)}, bf16[16,8,128,128]{3,2,1,0:T(8,128)(2,1)}, f32[16,8]{1,0:T(8,128)S(1)}, f32[16,8,128,128]{3,2,1,0:T(8,128)}) while((s32[]{:T(128)}, f32[8,128,128]{2,1,0:T(8,128)S(1)}, bf16[16,8,128,128]{3,2,1,0:T(8,128)(2,1)}, f32[16,8]{1,0:T(8,128)S(1)}, ...), condition=%wide.region_10.13_spmd.clone.clone, body=%wide.region_9.12_spmd.clone.sunk.clone | while | flops 524291 | bytes 2359484 | solution.py:34
  385.1 1.2 bitcast_add_fusion.4
  387.0 1.2 bitcast_add_fusion.4
  388.9 1.2 bitcast_add_fusion.4
  390.1 0.8 bitcast_dynamic-update-slice_fusion.3
  390.9 1.2 bitcast_add_fusion.4
  392.8 1.2 bitcast_add_fusion.4
  394.0 0.8 bitcast_dynamic-update-slice_fusion.3
  394.7 1.2 bitcast_add_fusion.4
  396.7 1.2 bitcast_add_fusion.4
  397.9 0.8 bitcast_dynamic-update-slice_fusion.3
  398.6 1.2 bitcast_add_fusion.4
  400.5 1.2 bitcast_add_fusion.4
  401.7 0.8 bitcast_dynamic-update-slice_fusion.3
  402.5 1.2 bitcast_add_fusion.4
  403.7 0.8 bitcast_dynamic-update-slice_fusion.3
  404.4 1.2 bitcast_add_fusion.4
  406.4 1.2 bitcast_add_fusion.4
  408.3 1.2 bitcast_add_fusion.4
  410.2 1.2 bitcast_add_fusion.4
  412.2 1.2 bitcast_add_fusion.4
  414.1 1.2 bitcast_add_fusion.4
  415.3 11.0 %fusion.5 = f32[16,8,128,128]{3,2,1,0:T(8,128)} fusion(bf16[16,128,8,128]{1,3,2,0:T(8,128)(2,1)} %bitcast.103, f32[16,8,128]{2,1,0:T(8,128)S(1)} %copy.161, pred[16,128,128]{2,1,0:T(8,128)(4,1)S(1)} %compare_and_fusion, bf16[16,128,8,128]{1,3,2,0:T(8,128)(2,1)} %bitcast.87, bf16[16,128,8,128]{1,3,2,0:T(8,128)(2,1)} %bitcast.105), kind=kOutput, calls=%fused_computation.28 | convolution fusion | flops 1084227584 | bytes 21299200 | tf_op jit(solution)/shard_map/nhts,nshd->nthd/dot_general | solution.py:57
  426.3 8.4 %fusion.9 = f32[16,8,128,128]{3,2,1,0:T(8,128)} fusion(bf16[16,128,8,128]{1,3,2,0:T(8,128)(2,1)} %bitcast.88, f32[16,128,8]{1,2,0:T(8,128)S(1)} %copy.171, bf16[16,8,128,128]{3,2,1,0:T(8,128)(2,1)} %get-tuple-element.61), kind=kOutput, calls=%fused_computation.31 | convolution fusion | flops 543162368 | bytes 16842752 | tf_op jit(solution)/shard_map/nthd,nhde->nthe/dot_general | solution.py:61
  434.7 85.4 %while.27 = (s32[]{:T(128)}, f32[8,128,128]{2,1,0:T(8,128)}, f32[8,128,128]{2,1,0:T(8,128)S(1)}, f32[8]{0:T(128)S(1)}, f32[8,128,128]{2,1,0:T(8,128)S(1)}) while((s32[]{:T(128)}, f32[8,128,128]{2,1,0:T(8,128)}, f32[8,128,128]{2,1,0:T(8,128)S(1)}, f32[8]{0:T(128)S(1)}, f32[8,128,128]{2,1,0:T(8,128)S(1)}) %tuple.63), condition=%wide.region_14.17_spmd.clone, body=%wide.region_13.16_spmd.sunk.clone | while | flops 262146 | bytes 5767329 | solution.py:77
  434.7 1.9 collective-permute-start
  436.6 9.5 %collective-permute-done = f32[8,128,128]{2,1,0:T(8,128)S(1)} collective-permute-done((f32[8,128,128]{2,1,0:T(8,128)S(1)}, f32[8,128,128]{2,1,0:T(8,128)S(1)}, u32[]{:S(2)}, u32[]{:S(2)}) %collective-permute-start) | collective-permute-done | bytes 524320 | tf_op jit(solution)/shard_map/while/body/eval_jaxpr/ppermute | solution.py:12
  446.9 1.9 collective-permute-start
  448.8 9.5 %collective-permute-done = f32[8,128,128]{2,1,0:T(8,128)S(1)} collective-permute-done((f32[8,128,128]{2,1,0:T(8,128)S(1)}, f32[8,128,128]{2,1,0:T(8,128)S(1)}, u32[]{:S(2)}, u32[]{:S(2)}) %collective-permute-start) | collective-permute-done | bytes 524320 | tf_op jit(solution)/shard_map/while/body/eval_jaxpr/ppermute | solution.py:12
  459.1 1.9 collective-permute-start
  461.0 9.5 %collective-permute-done = f32[8,128,128]{2,1,0:T(8,128)S(1)} collective-permute-done((f32[8,128,128]{2,1,0:T(8,128)S(1)}, f32[8,128,128]{2,1,0:T(8,128)S(1)}, u32[]{:S(2)}, u32[]{:S(2)}) %collective-permute-start) | collective-permute-done | bytes 524320 | tf_op jit(solution)/shard_map/while/body/eval_jaxpr/ppermute | solution.py:12
  471.3 1.9 collective-permute-start
  473.2 9.5 %collective-permute-done = f32[8,128,128]{2,1,0:T(8,128)S(1)} collective-permute-done((f32[8,128,128]{2,1,0:T(8,128)S(1)}, f32[8,128,128]{2,1,0:T(8,128)S(1)}, u32[]{:S(2)}, u32[]{:S(2)}) %collective-permute-start) | collective-permute-done | bytes 524320 | tf_op jit(solution)/shard_map/while/body/eval_jaxpr/ppermute | solution.py:12
  483.5 1.9 collective-permute-start
  485.4 9.5 %collective-permute-done = f32[8,128,128]{2,1,0:T(8,128)S(1)} collective-permute-done((f32[8,128,128]{2,1,0:T(8,128)S(1)}, f32[8,128,128]{2,1,0:T(8,128)S(1)}, u32[]{:S(2)}, u32[]{:S(2)}) %collective-permute-start) | collective-permute-done | bytes 524320 | tf_op jit(solution)/shard_map/while/body/eval_jaxpr/ppermute | solution.py:12
  495.7 1.9 collective-permute-start
  497.6 9.5 %collective-permute-done = f32[8,128,128]{2,1,0:T(8,128)S(1)} collective-permute-done((f32[8,128,128]{2,1,0:T(8,128)S(1)}, f32[8,128,128]{2,1,0:T(8,128)S(1)}, u32[]{:S(2)}, u32[]{:S(2)}) %collective-permute-start) | collective-permute-done | bytes 524320 | tf_op jit(solution)/shard_map/while/body/eval_jaxpr/ppermute | solution.py:12
  507.9 1.9 collective-permute-start
  509.8 9.5 %collective-permute-done = f32[8,128,128]{2,1,0:T(8,128)S(1)} collective-permute-done((f32[8,128,128]{2,1,0:T(8,128)S(1)}, f32[8,128,128]{2,1,0:T(8,128)S(1)}, u32[]{:S(2)}, u32[]{:S(2)}) %collective-permute-start) | collective-permute-done | bytes 524320 | tf_op jit(solution)/shard_map/while/body/eval_jaxpr/ppermute | solution.py:12
  520.1 12.6 %multiply_reduce_fusion = (f32[16,128]{1,0:T(8,128)S(1)}, f32[16,128,8,128]{1,3,2,0:T(8,128)}) fusion(bf16[16,128,8,128]{1,3,2,0:T(8,128)(2,1)} %bitcast.89, f32[16,128,8]{1,2,0:T(8,128)S(1)} %copy.178, f32[8,128,128]{2,1,0:T(8,128)} %get-tuple-element.63, f32[16,8,128,128]{3,2,1,0:T(8,128)} %fusion.5, f32[16,8,128,128]{3,2,1,0:T(8,128)} %fusion.9), kind=kOutput, calls=%fused_computation.25 | convolution fusion | flops 551680000 | bytes 29958144 | tf_op jit(solution)/shard_map/nthd,hde->nthe/dot_general | solution.py:149
  532.7 9.3 %copy.181 = f32[16,128,8,128]{3,2,1,0:T(8,128)} copy(f32[16,128,8,128]{1,3,2,0:T(8,128)} %get-tuple-element.144) | data formatting | bytes 16777216 | tf_op jit(solution)/shard_map/add | solution.py:152
  542.0 12.1 %psum.7 = f32[2048]{0:T(1024)S(1)} all-reduce(f32[2048]{0:T(1024)S(1)} %bitcast.109), channel_id=1, replica_groups=mesh['ctx'=8,'head'=4] {'head'}, use_global_device_ids=true, to_apply=%region_17.20 | all-reduce | flops 2048 | bytes 16384 | tf_op jit(solution)/shard_map/psum | solution.py:153
  554.1 6.8 %fusion.4 = bf16[2048,1024]{1,0:T(8,128)(2,1)} fusion(f32[256,8,8,128]{3,2,1,0:T(8,128)} %bitcast.90, f32[1024]{0:T(1024)S(1)} %copy-done.3, f32[2048]{0:T(1024)S(1)} %add_rsqrt_fusion), kind=kLoop, calls=%fused_computation.20 | loop fusion | flops 6291456 | bytes 12595200 | tf_op jit(solution)/shard_map/convert_element_type | solution.py:156
  (138 shorter events, 24.0 us)
Async XLA Ops:
  0.0 1.5 copy-start
  2.8 42.1 %all-to-all-start.3 = ((bf16[8,512,8]{1,2,0:T(8,128)(2,1)}), bf16[8,512,8]{1,2,0:T(8,128)(2,1)S(1)}, u32[]{:S(2)}, u32[]{:S(2)}) async-start(bf16[8,512,8]{1,2,0:T(8,128)(2,1)} %select_select_fusion.3), calls=%async_computation.3 | async-start | bytes 131072 | tf_op jit(solution)/shard_map/all_to_all | solution.py:132
  44.9 98.9 %slice-start = ((s8[8388608]{0:T(1024)(128)(4,1)}), s8[4194304]{0:T(1024)(128)(4,1)S(1)}, s32[]{:S(2)}) async-start(s8[8388608]{0:T(1024)(128)(4,1)} %bitcast.92), calls=%async_computation.4 | async-start | bytes 8388608
  44.9 98.9 %slice-start.1 = ((s8[8388608]{0:T(1024)(128)(4,1)}), s8[4194304]{0:T(1024)(128)(4,1)S(1)}, s32[]{:S(2)}) async-start(s8[8388608]{0:T(1024)(128)(4,1)} %bitcast.92), calls=%async_computation.5 | async-start | bytes 8388608
  241.2 6.6 %copy-start.5 = (s32[128]{0:T(128)S(1)}, s32[128]{0:T(128)}, u32[]{:S(2)}) copy-start(s32[128]{0:T(128)} %param.21) | copy-start | bytes 1540
  241.2 6.8 %copy-start.4 = (s32[16]{0:T(128)S(1)}, s32[16]{0:T(128)}, u32[]{:S(2)}) copy-start(s32[16]{0:T(128)} %param.20) | copy-start | bytes 196
  241.2 99.2 %all-to-all-start = ((bf16[8,512,1024]{2,1,0:T(8,128)(2,1)}), bf16[8,512,1024]{2,1,0:T(8,128)(2,1)}, u32[]{:S(2)}, u32[]{:S(2)}) async-start(bf16[8,512,1024]{2,1,0:T(8,128)(2,1)} %bitcast.91), calls=%async_computation | async-start | bytes 16777216 | tf_op jit(solution)/shard_map/all_to_all | solution.py:131
  434.7 11.4 %collective-permute-start = (f32[8,128,128]{2,1,0:T(8,128)S(1)}, f32[8,128,128]{2,1,0:T(8,128)S(1)}, u32[]{:S(2)}, u32[]{:S(2)}) collective-permute-start(f32[8,128,128]{2,1,0:T(8,128)S(1)} %get-tuple-element.253), channel_id=1, source_target_pairs={{0,4},{4,8},{8,12},{12,16},{16,20},{20,24},{24,28},{1,5},{5,9},{9,... | collective-permute-start | bytes 1572872 | tf_op jit(solution)/shard_map/while/body/eval_jaxpr/ppermute | solution.py:12
  446.0 0.8 copy-start.2
  446.9 11.4 %collective-permute-start = (f32[8,128,128]{2,1,0:T(8,128)S(1)}, f32[8,128,128]{2,1,0:T(8,128)S(1)}, u32[]{:S(2)}, u32[]{:S(2)}) collective-permute-start(f32[8,128,128]{2,1,0:T(8,128)S(1)} %get-tuple-element.253), channel_id=1, source_target_pairs={{0,4},{4,8},{8,12},{12,16},{16,20},{20,24},{24,28},{1,5},{5,9},{9,... | collective-permute-start | bytes 1572872 | tf_op jit(solution)/shard_map/while/body/eval_jaxpr/ppermute | solution.py:12
  458.2 0.8 copy-start.2
  459.1 11.4 %collective-permute-start = (f32[8,128,128]{2,1,0:T(8,128)S(1)}, f32[8,128,128]{2,1,0:T(8,128)S(1)}, u32[]{:S(2)}, u32[]{:S(2)}) collective-permute-start(f32[8,128,128]{2,1,0:T(8,128)S(1)} %get-tuple-element.253), channel_id=1, source_target_pairs={{0,4},{4,8},{8,12},{12,16},{16,20},{20,24},{24,28},{1,5},{5,9},{9,... | collective-permute-start | bytes 1572872 | tf_op jit(solution)/shard_map/while/body/eval_jaxpr/ppermute | solution.py:12
  470.5 0.8 copy-start.2
  471.3 11.4 %collective-permute-start = (f32[8,128,128]{2,1,0:T(8,128)S(1)}, f32[8,128,128]{2,1,0:T(8,128)S(1)}, u32[]{:S(2)}, u32[]{:S(2)}) collective-permute-start(f32[8,128,128]{2,1,0:T(8,128)S(1)} %get-tuple-element.253), channel_id=1, source_target_pairs={{0,4},{4,8},{8,12},{12,16},{16,20},{20,24},{24,28},{1,5},{5,9},{9,... | collective-permute-start | bytes 1572872 | tf_op jit(solution)/shard_map/while/body/eval_jaxpr/ppermute | solution.py:12
  482.7 0.8 copy-start.2
  483.5 11.4 %collective-permute-start = (f32[8,128,128]{2,1,0:T(8,128)S(1)}, f32[8,128,128]{2,1,0:T(8,128)S(1)}, u32[]{:S(2)}, u32[]{:S(2)}) collective-permute-start(f32[8,128,128]{2,1,0:T(8,128)S(1)} %get-tuple-element.253), channel_id=1, source_target_pairs={{0,4},{4,8},{8,12},{12,16},{16,20},{20,24},{24,28},{1,5},{5,9},{9,... | collective-permute-start | bytes 1572872 | tf_op jit(solution)/shard_map/while/body/eval_jaxpr/ppermute | solution.py:12
  494.9 0.8 copy-start.2
  495.7 11.4 %collective-permute-start = (f32[8,128,128]{2,1,0:T(8,128)S(1)}, f32[8,128,128]{2,1,0:T(8,128)S(1)}, u32[]{:S(2)}, u32[]{:S(2)}) collective-permute-start(f32[8,128,128]{2,1,0:T(8,128)S(1)} %get-tuple-element.253), channel_id=1, source_target_pairs={{0,4},{4,8},{8,12},{12,16},{16,20},{20,24},{24,28},{1,5},{5,9},{9,... | collective-permute-start | bytes 1572872 | tf_op jit(solution)/shard_map/while/body/eval_jaxpr/ppermute | solution.py:12
  507.1 0.8 copy-start.2
  507.9 11.4 %collective-permute-start = (f32[8,128,128]{2,1,0:T(8,128)S(1)}, f32[8,128,128]{2,1,0:T(8,128)S(1)}, u32[]{:S(2)}, u32[]{:S(2)}) collective-permute-start(f32[8,128,128]{2,1,0:T(8,128)S(1)} %get-tuple-element.253), channel_id=1, source_target_pairs={{0,4},{4,8},{8,12},{12,16},{16,20},{20,24},{24,28},{1,5},{5,9},{9,... | collective-permute-start | bytes 1572872 | tf_op jit(solution)/shard_map/while/body/eval_jaxpr/ppermute | solution.py:12
  519.3 0.8 copy-start.2
  532.7 21.4 %copy-start.3 = (f32[1024]{0:T(1024)S(1)}, f32[1024]{0:T(1024)}, u32[]{:S(2)}) copy-start(f32[1024]{0:T(1024)} %param.19) | copy-start | bytes 12292
  554.1 6.8 %copy-start.1 = (bf16[2048,8]{0,1:T(8,128)(2,1)S(1)}, bf16[2048,8]{0,1:T(8,128)(2,1)}, u32[]{:S(2)}) copy-start(bf16[2048,8]{0,1:T(8,128)(2,1)} %param.18) | copy-start | bytes 98308
where the time goes:
time: 563 us; the launch traced here: 561 us
  blocking collectives  208 us (37%)
  waiting for transfers between devices  110 us (20%)
  other arithmetic  94.2 us (17%)
  local copies, waits for them, and re-layouts  81.3 us (14%)
  matrix products  41.7 us (7%)
  starting transfers between devices  24 us (4%)
    all_to_all x1, blocking collectives, body(): lax.all_to_all(outgoing(key_rows), 'ctx', split_axis=0, concat_axis=0, ti...  98.8 us
    all_to_all x1, blocking collectives, body(): lax.all_to_all(outgoing(queries), 'ctx', split_axis=0, concat_axis=0, til...  97.5 us
    ppermute x7, waiting for transfers between devices, from_behind(): return lax.ppermute(x, axis, pairs)  66.3 us
    all_to_all x1, waiting for transfers between devices, body(): lax.all_to_all(outgoing(value_rows), 'ctx', split_axis=0, concat_axis=0,...  43.7 us
    another operation x1, other arithmetic, state_pass(): block_log = jnp.cumsum(decay_blocks.astype(jnp.float32), axis=1)  23.3 us
    gather x4, local copies, waits for them, and re-layouts, outgoing(): picked = jnp.take(values.reshape(blocks, BLOCK, columns), source, axis=0)  21.9 us
    gather x4, local copies, waits for them, and re-layouts, arriving(): jnp.take(values.reshape(devices * capacity, BLOCK, values.shape[2]), colu...  19.1 us
    add x16, other arithmetic, advance(): return (factor[:, None, None] * state + term, state)  18.5 us
  transfers between devices with their start and end apart: 9, of which 8 were waited for; matrix products, arithmetic and copies ran while one was open for 15% of the time, Pallas kernels for 0%

commit v1 on v0

--- a/solution.py
+++ b/solution.py
@@ -1,9 +1,386 @@
+import functools
+
 import jax
 import jax.numpy as jnp
 from jax import lax
+from jax.experimental import pallas as pl
+from jax.experimental.pallas import tpu as pltpu
 from jax.sharding import PartitionSpec as P
 
 BLOCK = 128
+MESH = pl.DeviceIdType.MESH
+ORDER = (4, 2, 6, 1, 5, 3, 7)
+ARRAYS = 3
+
+
+def flipped(me, bits):
+    high, mid, low = me // 4, (me // 2) % 2, me % 2
+    return (
+        4 * ((high + bits // 4) % 2) + 2 * ((mid + bits // 2 % 2) % 2) + (low + bits % 2) % 2
+    )
+
+
+def contract(a, b, dim_a, dim_b):
+    return lax.dot_general(
+        a, b, (((dim_a,), (dim_b,)), ((), ())), preferred_element_type=jnp.float32
+    )
+
+
+def attention_kernel(
+    peers,
+    q_hbm,
+    k_hbm,
+    v_hbm,
+    log_ref,
+    meta_ref,
+    source_ref,
+    out_hbm,
+    total_ref,
+    q_all,
+    k_all,
+    v_all,
+    log_all,
+    intra,
+    own,
+    gate,
+    states,
+    out_all,
+    squares,
+    squares_in,
+    share_in,
+    send_sem,
+    recv_sem,
+    log_send,
+    log_recv,
+    out_send,
+    out_recv,
+    sq_send,
+    sq_recv,
+    share_send,
+    share_recv,
+):
+    ctx, head = peers
+    me = lax.axis_index("ctx")
+    plane = lax.axis_index("head")
+    blocks = log_ref.shape[1]
+    others = ORDER
+
+    barrier = pltpu.get_barrier_semaphore()
+    for bits in others:
+        pl.semaphore_signal(
+            barrier, inc=1, device_id=(flipped(me, bits), plane), device_id_type=MESH
+        )
+    for step in range(1, head):
+        pl.semaphore_signal(
+            barrier, inc=1, device_id=(me, (plane + step) % head), device_id_type=MESH
+        )
+    pl.semaphore_wait(barrier, ctx - 1 + head - 1)
+
+    sources = (k_hbm, v_hbm, q_hbm)
+    landings = (k_all, v_all, q_all)
+
+    def columns(index):
+        return pl.ds(pl.multiple_of(index * BLOCK, BLOCK), BLOCK)
+
+    def span(index):
+        return pl.ds(index * blocks, blocks)
+
+    def log_copy(bits):
+        there = flipped(me, bits)
+        return pltpu.make_async_remote_copy(
+            src_ref=log_ref.at[there],
+            dst_ref=log_all.at[me],
+            send_sem=log_send.at[bits],
+            recv_sem=log_recv.at[bits],
+            device_id=(there, plane),
+            device_id_type=MESH,
+        )
+
+    def row_copy(bits, which):
+        there = flipped(me, bits)
+        return pltpu.make_async_remote_copy(
+            src_ref=sources[which].at[:, :, columns(there)],
+            dst_ref=landings[which].at[span(me)],
+            send_sem=send_sem.at[bits, which],
+            recv_sem=recv_sem.at[bits, which],
+            device_id=(there, plane),
+            device_id_type=MESH,
+        )
+
+    def row_landing(bits, which):
+        there = flipped(me, bits)
+        return pltpu.make_async_remote_copy(
+            src_ref=sources[which].at[:, :, columns(there)],
+            dst_ref=landings[which].at[span(there)],
+            send_sem=send_sem.at[bits, which],
+            recv_sem=recv_sem.at[bits, which],
+            device_id=(there, plane),
+            device_id_type=MESH,
+        )
+
+    def log_landing(bits):
+        there = flipped(me, bits)
+        return pltpu.make_async_remote_copy(
+            src_ref=log_ref.at[there],
+            dst_ref=log_all.at[there],
+            send_sem=log_send.at[bits],
+            recv_sem=log_recv.at[bits],
+            device_id=(there, plane),
+            device_id_type=MESH,
+        )
+
+    kept = [
+        pltpu.make_async_copy(
+            sources[which].at[:, :, columns(me)],
+            landings[which].at[span(me)],
+            recv_sem.at[0, which],
+        )
+        for which in range(ARRAYS)
+    ]
+    kept.append(pltpu.make_async_copy(log_ref.at[me], log_all.at[me], log_recv.at[0]))
+    for copy in kept:
+        copy.start()
+    for bits in others:
+        log_copy(bits).start()
+    for bits in others:
+        for which in range(ARRAYS):
+            row_copy(bits, which).start()
+
+    sub = lax.broadcasted_iota(jnp.int32, (BLOCK, BLOCK), 0)
+    lane = lax.broadcasted_iota(jnp.int32, (BLOCK, BLOCK), 1)
+
+    def local_block(there, index):
+        log_row = log_all[there, pl.ds(index, 1), :]
+        across = jnp.broadcast_to(log_row, (BLOCK, BLOCK))
+        down = jnp.transpose(across)
+        block = there * blocks + index
+        begins = meta_ref[block, 0:1, :]
+        broken_at = meta_ref[block, 1:2, :]
+        last_begin = meta_ref[block, 2:3, :]
+        queries = q_all[block]
+        keys = k_all[block]
+        values = v_all[block]
+        scores = contract(keys, queries, 1, 1)
+        allowed = (sub >= begins) & (sub <= lane)
+        weight = jnp.where(allowed, jnp.exp(jnp.minimum(across - down, 0.0)), 0.0)
+        weights = (scores * weight).astype(jnp.bfloat16)
+        intra[block] = contract(weights, values, 0, 0)
+        total = jnp.broadcast_to(log_row[:, BLOCK - 1 :], (1, BLOCK))
+        keep = jnp.where(sub >= last_begin, jnp.exp(jnp.minimum(total - down, 0.0)), 0.0)
+        decayed = (keys.astype(jnp.float32) * keep).astype(jnp.bfloat16)
+        own[block] = contract(decayed, values, 0, 0)
+        gate[block] = jnp.where(last_begin < 0, jnp.exp(total), 0.0)
+        reach = jnp.where(sub < broken_at, jnp.exp(down), 0.0)
+        q_all[block] = (queries.astype(jnp.float32) * reach).astype(jnp.bfloat16)
+
+    def local_blocks(there):
+        def several(step, carry):
+            for extra in range(4):
+                local_block(there, step * 4 + extra)
+            return carry
+
+        lax.fori_loop(0, blocks // 4, several, 0)
+
+    for copy in kept:
+        copy.wait()
+    local_blocks(me)
+    for bits in others:
+        log_landing(bits).wait_recv()
+        for which in range(ARRAYS):
+            row_landing(bits, which).wait_recv()
+        local_blocks(flipped(me, bits))
+
+    def advance(step, state):
+        for extra in range(4):
+            place = step * 4 + extra
+            block = source_ref[place]
+            states[place] = state.astype(jnp.bfloat16)
+            state = gate[block] * state + own[block]
+        return state
+
+    lax.fori_loop(0, ctx * blocks // 4, advance, jnp.zeros((BLOCK, BLOCK), jnp.float32))
+
+    ones = jnp.ones((8, BLOCK), jnp.bfloat16)
+
+    def out_copy(bits):
+        there = flipped(me, bits)
+        return pltpu.make_async_remote_copy(
+            src_ref=out_all.at[span(there)],
+            dst_ref=out_hbm.at[:, :, columns(me)],
+            send_sem=out_send.at[bits],
+            recv_sem=out_recv.at[bits],
+            device_id=(there, plane),
+            device_id_type=MESH,
+        )
+
+    def out_landing(bits):
+        there = flipped(me, bits)
+        return pltpu.make_async_remote_copy(
+            src_ref=out_all.at[span(there)],
+            dst_ref=out_hbm.at[:, :, columns(there)],
+            send_sem=out_send.at[bits],
+            recv_sem=out_recv.at[bits],
+            device_id=(there, plane),
+            device_id_type=MESH,
+        )
+
+    def sq_copy(bits):
+        there = flipped(me, bits)
+        return pltpu.make_async_remote_copy(
+            src_ref=squares.at[there],
+            dst_ref=squares_in.at[me],
+            send_sem=sq_send.at[bits],
+            recv_sem=sq_recv.at[bits],
+            device_id=(there, plane),
+            device_id_type=MESH,
+        )
+
+    def sq_landing(bits):
+        there = flipped(me, bits)
+        return pltpu.make_async_remote_copy(
+            src_ref=squares.at[there],
+            dst_ref=squares_in.at[there],
+            send_sem=sq_send.at[bits],
+            recv_sem=sq_recv.at[bits],
+            device_id=(there, plane),
+            device_id_type=MESH,
+        )
+
+    def finish(there):
+        def several(step, carry):
+            for extra in range(4):
+                index = step * 4 + extra
+                place = there * blocks + index
+                block = source_ref[place]
+                result = intra[block] + contract(q_all[block], states[place], 1, 0)
+                out_all[place] = result.astype(jnp.bfloat16)
+                summed = contract(ones, (result * result).astype(jnp.bfloat16), 1, 1)
+                squares[there, pl.ds(index, 1), :] = summed[0:1]
+            return carry
+
+        lax.fori_loop(0, blocks // 4, several, 0)
+
+    for bits in others:
+        finish(flipped(me, bits))
+        out_copy(bits).start()
+        sq_copy(bits).start()
+    finish(me)
+    kept_out = pltpu.make_async_copy(
+        out_all.at[span(me)], out_hbm.at[:, :, columns(me)], out_recv.at[0]
+    )
+    kept_out.start()
+    summed = squares[me]
+    for bits in others:
+        sq_landing(bits).wait_recv()
+        summed = summed + squares_in[flipped(me, bits)]
+    share_in[plane] = summed
+
+    def share_copy(step, slot):
+        return pltpu.make_async_remote_copy(
+            src_ref=share_in.at[plane],
+            dst_ref=share_in.at[slot],
+            send_sem=share_send.at[step],
+            recv_sem=share_recv.at[step],
+            device_id=(me, (plane + step) % head),
+            device_id_type=MESH,
+        )
+
+    for step in range(1, head):
+        share_copy(step, plane).start()
+    total = summed
+    for step in range(1, head):
+        origin = (plane + head - step) % head
+        share_copy(step, origin).wait_recv()
+        total = total + share_in[origin]
+    total_ref[...] = total
+    kept_out.wait()
+    for bits in others:
+        out_landing(bits).wait_recv()
+    for bits in others:
+        log_copy(bits).wait_send()
+        for which in range(ARRAYS):
+            row_copy(bits, which).wait_send()
+        out_copy(bits).wait_send()
+        sq_copy(bits).wait_send()
+    for step in range(1, head):
+        share_copy(step, plane).wait_send()
+
+
+def by_head(queries, key_rows, value_rows, log_decay, norm_gain, doc_lengths, packing):
+    rows, width = queries.shape
+    heads = log_decay.shape[1]
+    blocks = rows // BLOCK
+    ctx = lax.axis_size("ctx")
+    head = lax.axis_size("head")
+    total_blocks = packing.shape[0]
+
+    order = jnp.arange(BLOCK)
+    lower = (order[:, None] >= order[None, :]).astype(jnp.bfloat16)
+    logs = jnp.einsum(
+        "ts,nsh->hnt",
+        lower,
+        log_decay.reshape(blocks, BLOCK, heads),
+        preferred_element_type=jnp.float32,
+    )
+    starts = jnp.cumsum(doc_lengths) - doc_lengths
+    base = packing * BLOCK
+    relative = starts[None, None, :] - base[:, None, None]
+    begins = jnp.max(jnp.where(relative <= order[None, :, None], relative, -(1 << 24)), axis=2)
+    broken_at = jnp.min(jnp.where(relative >= 0, relative, BLOCK), axis=2)
+    broken_at = jnp.broadcast_to(broken_at, begins.shape)
+    last_begin = jnp.broadcast_to(begins[:, -1:], begins.shape)
+    meta = jnp.stack([begins, broken_at, last_begin], axis=1)
+    places = jnp.arange(total_blocks, dtype=jnp.int32)
+    source = jnp.sum(
+        jnp.where(packing[None, :] == places[:, None], places[None, :], 0), axis=1
+    ).astype(jnp.int32)
+
+    def in_blocks(values):
+        return values.reshape(blocks, BLOCK, width)
+
+    any_spec = pl.BlockSpec(memory_space=pl.ANY)
+    vmem = pl.BlockSpec(memory_space=pltpu.VMEM)
+    dma = pltpu.SemaphoreType.DMA
+    out, squares = pl.pallas_call(
+        functools.partial(attention_kernel, (ctx, head)),
+        out_shape=(
+            jax.ShapeDtypeStruct((blocks, BLOCK, width), jnp.bfloat16),
+            jax.ShapeDtypeStruct((blocks, BLOCK), jnp.float32),
+        ),
+        in_specs=[any_spec] * 3 + [vmem, vmem, pl.BlockSpec(memory_space=pltpu.SMEM)],
+        out_specs=(any_spec, vmem),
+        scratch_shapes=[
+            pltpu.VMEM((total_blocks, BLOCK, BLOCK), jnp.bfloat16),
+            pltpu.VMEM((total_blocks, BLOCK, BLOCK), jnp.bfloat16),
+            pltpu.VMEM((total_blocks, BLOCK, BLOCK), jnp.bfloat16),
+            pltpu.VMEM((ctx, blocks, BLOCK), jnp.float32),
+            pltpu.VMEM((total_blocks, BLOCK, BLOCK), jnp.float32),
+            pltpu.VMEM((total_blocks, BLOCK, BLOCK), jnp.float32),
+            pltpu.VMEM((total_blocks, 1, BLOCK), jnp.float32),
+            pltpu.VMEM((total_blocks, BLOCK, BLOCK), jnp.bfloat16),
+            pltpu.VMEM((total_blocks, BLOCK, BLOCK), jnp.bfloat16),
+            pltpu.VMEM((ctx, blocks, BLOCK), jnp.float32),
+            pltpu.VMEM((ctx, blocks, BLOCK), jnp.float32),
+            pltpu.VMEM((head, blocks, BLOCK), jnp.float32),
+            dma((ctx, ARRAYS)),
+            dma((ctx, ARRAYS)),
+            dma((ctx,)),
+            dma((ctx,)),
+            dma((ctx,)),
+            dma((ctx,)),
+            dma((ctx,)),
+            dma((ctx,)),
+            dma((head,)),
+            dma((head,)),
+        ],
+        compiler_params=pltpu.CompilerParams(
+            collective_id=0, has_side_effects=True, vmem_limit_bytes=52 * 1024 * 1024
+        ),
+        name="attention_by_head",
+    )(in_blocks(queries), in_blocks(key_rows), in_blocks(value_rows), logs, meta, source)
+    scale = lax.rsqrt(squares / (width * head) + 1e-05)
+    normed = out.astype(jnp.float32) * scale[:, :, None] * norm_gain[None, None, :]
+    return normed.astype(jnp.bfloat16).reshape(rows, width)
 
 
 def from_behind(x, axis, by):
@@ -166,6 +543,7 @@
         P(),
         P(),
     )
+    one_head_each = mesh.shape["ctx"] == 8 and mesh.shape["head"] == 4
     return jax.shard_map(
-        body, mesh=mesh, in_specs=placed, out_specs=P("ctx", "head"), check_vma=False
-    )
+        by_head if one_head_each else body, mesh=mesh, in_specs=placed, out_specs=P("ctx", "head"), check_vma=False
+    )

time: 563 us -> 213 us (0.38)
  blocking collectives: 208 us -> 0 us
  Pallas kernels: 0 us -> 201 us
  waiting for transfers between devices: 110 us -> 0 us
  other arithmetic: 94.2 us -> 7.18 us
  local copies, waits for them, and re-layouts: 81.3 us -> 2.07 us
  matrix products: 41.7 us -> 0.14 us
  starting transfers between devices: 24 us -> 0 us
    pallas_call x0 -> x1, Pallas kernels: none -> 201 us  [by_head(): pl.pallas_call(functools.partial(attention_kernel, (ctx, head)), out_shap...]
    all_to_all x2 -> x0, blocking collectives: 196 us -> none  [the longest x1 98.8 us: body(): lax.all_to_all(outgoing(key_rows), 'ctx', split_axis=0, concat_axis=0, ti...]
    ppermute x7 -> x0, waiting for transfers between devices: 66.3 us -> none  [from_behind(): return lax.ppermute(x, axis, pairs)]
    all_to_all x2 -> x0, waiting for transfers between devices: 43.7 us -> none  [the longest x1 43.7 us: body(): lax.all_to_all(outgoing(value_rows), 'ctx', split_axis=0, concat_axis=0,...]
    gather x10 -> x0, local copies, waits for them, and re-layouts: 41.8 us -> none  [the longest x4 21.9 us: outgoing(): picked = jnp.take(values.reshape(blocks, BLOCK, columns), source, axis=0)]
    dot_general x4 -> x1, matrix products: 41.7 us -> 0.14 us  [by_head(): jnp.einsum('ts,nsh->hnt', lower, log_decay.reshape(blocks, BLOCK, heads),...]
    select_n x8 -> x0, other arithmetic: 27 us -> none  [the longest x2 17.2 us: outgoing(): kept = jnp.where(filled[:, None, None], picked, jnp.zeros((), values.dtype))]
    another operation x8 -> x3, other arithmetic: 23.8 us -> 0.33 us  [the longest x1 0.17 us: by_head(): meta = jnp.stack([begins, broken_at, last_begin], axis=1)]
  transfers between devices with their start and end apart: 9 -> 0, of which waited for: 8 -> 0; matrix products, arithmetic and copies ran while one was open for 15% -> 0% of each run, Pallas kernels for 0% -> 0%
where the time goes in v1:
time: 213 us; the launch traced here: 210 us
  Pallas kernels  201 us (94%)
  other arithmetic  7.18 us (3%)
    pallas_call x1, Pallas kernels, by_head(): pl.pallas_call(functools.partial(attention_kernel, (ctx, head)), out_shap...  201 us

profile of v1, /device:TPU:4, one launch (start us, length us, event | category | flops | bytes accessed | tf_op | source)
XLA Modules:
  0.0 210.2 jit_solution(12323702516753077188)
XLA Ops:
  0.0 0.0 copy-start
  0.0 0.8 copy-done
  0.8 0.7 broadcast_multiply_fusion
  1.4 0.8 select_reduce_fusion.1.source_ref
  2.2 0.7 copy.13
  3.0 0.1 reduce.1
  3.1 0.7 sub.33
  3.7 0.1 fusion.3
  3.8 0.1 broadcast_subtract_fusion
  3.9 0.5 select_reduce_fusion
  4.4 0.2 slice_reduce_fusion
  4.6 0.2 stack_broadcast_in_dim.5
  4.8 0.2 stack_broadcast_in_dim.4
  5.0 0.2 pad_add_fusion.meta_ref
  5.1 0.1 convolution_bitcast_fusion.log_ref
  5.3 0.0 copy-start.1
  5.3 200.7 %attention_by_head.1 = (bf16[16,128,1024]{2,1,0:T(8,128)(2,1)}, f32[16,128]{1,0:T(8,128)S(1)}) custom-call(bf16[16,128,1024]{2,1,0:T(8,128)(2,1)} %bitcast.13, bf16[16,128,1024]{2,1,0:T(8,128)(2,1)} %bitcast.14, bf16[16,128,1024]{2,1,0:T(8,128)(2,1)} %bitcast.15, f32[8,16,128]{2,1,0:T(8,128)S(1)} %convolution_bitcast_fusion.log_ref, ...), custom_call_target="tpu_custom_call" | custom-call | tf_op jit(solution)/shard_map/attention_by_head/pallas_call | solution.py:344
  206.0 0.0 copy-done.1
  206.1 4.1 %multiply_convert_fusion = bf16[16,128,1024]{2,1,0:T(8,128)(2,1)} fusion(bf16[16,128,1024]{2,1,0:T(8,128)(2,1)} %get-tuple-element.7, f32[1024]{0:T(1024)S(1)} %copy-done.1, f32[16,128]{1,0:T(8,128)S(1)} %add_rsqrt_fusion), kind=kLoop, calls=%fused_computation | loop fusion | flops 8388608 | bytes 8400896 | tf_op jit(solution)/shard_map/convert_element_type | solution.py:383
  (2 shorter events, 0.0 us)
Async XLA Ops:
  0.0 0.8 copy-start
  5.3 200.8 %copy-start.1 = (f32[1024]{0:T(1024)S(1)}, f32[1024]{0:T(1024)}, u32[]{:S(2)}) copy-start(f32[1024]{0:T(1024)} %param.11) | copy-start | bytes 12292

commit v2 on v1

--- a/solution.py
+++ b/solution.py
@@ -11,6 +11,19 @@
 MESH = pl.DeviceIdType.MESH
 ORDER = (4, 2, 6, 1, 5, 3, 7)
 ARRAYS = 3
+AHEAD = 2
+
+
+def stage_list(blocks):
+    stages = []
+    slot = 0
+    for low in range(0, blocks, 4):
+        stages.append(((0, 1), low, 4, slot))
+        slot += 2
+    for low in range(0, blocks, 2):
+        stages.append(((2,), low, 2, slot))
+        slot += 1
+    return stages
 
 
 def flipped(me, bits):
@@ -32,7 +45,8 @@
     k_hbm,
     v_hbm,
     log_ref,
-    meta_ref,
+    length_ref,
+    packing_ref,
     source_ref,
     out_hbm,
     total_ref,
@@ -40,6 +54,7 @@
     k_all,
     v_all,
     log_all,
+    meta,
     intra,
     own,
     gate,
@@ -50,6 +65,7 @@
     share_in,
     send_sem,
     recv_sem,
+    kept_sem,
     log_send,
     log_recv,
     out_send,
@@ -63,6 +79,7 @@
     me = lax.axis_index("ctx")
     plane = lax.axis_index("head")
     blocks = log_ref.shape[1]
+    total_blocks = ctx * blocks
     others = ORDER
 
     barrier = pltpu.get_barrier_semaphore()
@@ -76,119 +93,142 @@
         )
     pl.semaphore_wait(barrier, ctx - 1 + head - 1)
 
-    sources = (k_hbm, v_hbm, q_hbm)
-    landings = (k_all, v_all, q_all)
+    pairs = ((k_hbm, k_all), (v_hbm, v_all), (q_hbm, q_all))
+    stages = stage_list(blocks)
 
     def columns(index):
         return pl.ds(pl.multiple_of(index * BLOCK, BLOCK), BLOCK)
 
-    def span(index):
-        return pl.ds(index * blocks, blocks)
-
-    def log_copy(bits):
-        there = flipped(me, bits)
+    def span(index, low=0, count=blocks):
+        return pl.ds(index * blocks + low, count)
+
+    def remote(source, target, send, recv, there):
         return pltpu.make_async_remote_copy(
-            src_ref=log_ref.at[there],
-            dst_ref=log_all.at[me],
-            send_sem=log_send.at[bits],
-            recv_sem=log_recv.at[bits],
+            src_ref=source,
+            dst_ref=target,
+            send_sem=send,
+            recv_sem=recv,
             device_id=(there, plane),
             device_id_type=MESH,
         )
 
-    def row_copy(bits, which):
+    def row_copies(stage, bits, arriving):
+        arrays, low, count, slot = stages[stage]
         there = flipped(me, bits)
-        return pltpu.make_async_remote_copy(
-            src_ref=sources[which].at[:, :, columns(there)],
-            dst_ref=landings[which].at[span(me)],
-            send_sem=send_sem.at[bits, which],
-            recv_sem=recv_sem.at[bits, which],
-            device_id=(there, plane),
-            device_id_type=MESH,
-        )
-
-    def row_landing(bits, which):
+        origin = there if arriving else me
+        return [
+            remote(
+                pairs[which][0].at[pl.ds(low, count), :, columns(there)],
+                pairs[which][1].at[span(origin, low, count)],
+                send_sem.at[slot + extra, bits],
+                recv_sem.at[slot + extra, bits],
+                there,
+            )
+            for extra, which in enumerate(arrays)
+        ]
+
+    def log_copy(bits, arriving):
         there = flipped(me, bits)
-        return pltpu.make_async_remote_copy(
-            src_ref=sources[which].at[:, :, columns(there)],
-            dst_ref=landings[which].at[span(there)],
-            send_sem=send_sem.at[bits, which],
-            recv_sem=recv_sem.at[bits, which],
-            device_id=(there, plane),
-            device_id_type=MESH,
-        )
-
-    def log_landing(bits):
-        there = flipped(me, bits)
-        return pltpu.make_async_remote_copy(
-            src_ref=log_ref.at[there],
-            dst_ref=log_all.at[there],
-            send_sem=log_send.at[bits],
-            recv_sem=log_recv.at[bits],
-            device_id=(there, plane),
-            device_id_type=MESH,
-        )
-
+        origin = there if arriving else me
+        return remote(
+            log_ref.at[there], log_all.at[origin], log_send.at[bits], log_recv.at[bits], there
+        )
+
+    def begin(stage):
+        for bits in others:
+            for copy in row_copies(stage, bits, False):
+                copy.start()
+
+    def sent(stage):
+        for bits in others:
+            for copy in row_copies(stage, bits, False):
+                copy.wait_send()
+
+    def arrived(stage):
+        for bits in others:
+            for copy in row_copies(stage, bits, True):
+                copy.wait_recv()
+
+    for bits in others:
+        log_copy(bits, False).start()
+    for stage in range(AHEAD):
+        begin(stage)
     kept = [
         pltpu.make_async_copy(
-            sources[which].at[:, :, columns(me)],
-            landings[which].at[span(me)],
-            recv_sem.at[0, which],
-        )
-        for which in range(ARRAYS)
+            source.at[:, :, columns(me)], landing.at[span(me)], kept_sem.at[index]
+        )
+        for index, (source, landing) in enumerate(pairs)
     ]
-    kept.append(pltpu.make_async_copy(log_ref.at[me], log_all.at[me], log_recv.at[0]))
+    kept.append(pltpu.make_async_copy(log_ref.at[me], log_all.at[me], kept_sem.at[ARRAYS]))
     for copy in kept:
         copy.start()
-    for bits in others:
-        log_copy(bits).start()
-    for bits in others:
-        for which in range(ARRAYS):
-            row_copy(bits, which).start()
 
     sub = lax.broadcasted_iota(jnp.int32, (BLOCK, BLOCK), 0)
     lane = lax.broadcasted_iota(jnp.int32, (BLOCK, BLOCK), 1)
-
-    def local_block(there, index):
-        log_row = log_all[there, pl.ds(index, 1), :]
-        across = jnp.broadcast_to(log_row, (BLOCK, BLOCK))
-        down = jnp.transpose(across)
-        block = there * blocks + index
-        begins = meta_ref[block, 0:1, :]
-        broken_at = meta_ref[block, 1:2, :]
-        last_begin = meta_ref[block, 2:3, :]
-        queries = q_all[block]
-        keys = k_all[block]
-        values = v_all[block]
-        scores = contract(keys, queries, 1, 1)
-        allowed = (sub >= begins) & (sub <= lane)
-        weight = jnp.where(allowed, jnp.exp(jnp.minimum(across - down, 0.0)), 0.0)
-        weights = (scores * weight).astype(jnp.bfloat16)
-        intra[block] = contract(weights, values, 0, 0)
-        total = jnp.broadcast_to(log_row[:, BLOCK - 1 :], (1, BLOCK))
-        keep = jnp.where(sub >= last_begin, jnp.exp(jnp.minimum(total - down, 0.0)), 0.0)
-        decayed = (keys.astype(jnp.float32) * keep).astype(jnp.bfloat16)
-        own[block] = contract(decayed, values, 0, 0)
-        gate[block] = jnp.where(last_begin < 0, jnp.exp(total), 0.0)
-        reach = jnp.where(sub < broken_at, jnp.exp(down), 0.0)
-        q_all[block] = (queries.astype(jnp.float32) * reach).astype(jnp.bfloat16)
-
-    def local_blocks(there):
-        def several(step, carry):
-            for extra in range(4):
-                local_block(there, step * 4 + extra)
-            return carry
-
-        lax.fori_loop(0, blocks // 4, several, 0)
-
+    along = lax.broadcasted_iota(jnp.int32, (1, BLOCK), 1)
+
+    starts = [jnp.int32(0)]
+    for index in range(length_ref.shape[0] - 1):
+        starts.append(starts[-1] + length_ref[index])
+
+    def mark(block, carry):
+        base = packing_ref[block] * BLOCK
+        begins = jnp.full((1, BLOCK), -(1 << 24), jnp.int32)
+        broken_at = jnp.full((1, BLOCK), BLOCK, jnp.int32)
+        for start in starts:
+            relative = jnp.broadcast_to(start - base, (1, BLOCK))
+            begins = jnp.maximum(begins, jnp.where(relative <= along, relative, -(1 << 24)))
+            broken_at = jnp.minimum(broken_at, jnp.where(relative >= 0, relative, BLOCK))
+        meta[block, 0:1, :] = begins
+        meta[block, 1:2, :] = broken_at
+        meta[block, 2:3, :] = jnp.broadcast_to(begins[:, BLOCK - 1 :], (1, BLOCK))
+        return carry
+
+    lax.fori_loop(0, total_blocks, mark, 0)
     for copy in kept:
         copy.wait()
-    local_blocks(me)
-    for bits in others:
-        log_landing(bits).wait_recv()
-        for which in range(ARRAYS):
-            row_landing(bits, which).wait_recv()
-        local_blocks(flipped(me, bits))
+    for bits in others:
+        log_copy(bits, True).wait_recv()
+
+    def down(row):
+        return jnp.transpose(jnp.broadcast_to(row, (BLOCK, BLOCK)))
+
+    def key_block(there, index):
+        block = there * blocks + index
+        log_row = log_all[there, index : index + 1, :]
+        last_begin = meta[block, 2:3, :]
+        total = jnp.broadcast_to(log_row[:, BLOCK - 1 :], (1, BLOCK))
+        keep = jnp.where(along >= last_begin, jnp.exp(total - log_row), 0.0)
+        decayed = (k_all[block].astype(jnp.float32) * down(keep)).astype(jnp.bfloat16)
+        own[block] = contract(decayed, v_all[block], 0, 0)
+        gate[block] = jnp.where(last_begin < 0, jnp.exp(total), 0.0)
+
+    def query_block(there, index):
+        block = there * blocks + index
+        log_row = log_all[there, index : index + 1, :]
+        begins = meta[block, 0:1, :]
+        broken_at = meta[block, 1:2, :]
+        queries = q_all[block]
+        scores = contract(k_all[block], queries, 1, 1)
+        allowed = (sub >= begins) & (sub <= lane)
+        gaps = jnp.minimum(log_row - down(log_row), 0.0)
+        weights = jnp.where(allowed, scores * jnp.exp(gaps), 0.0).astype(jnp.bfloat16)
+        intra[block] = contract(weights, v_all[block], 0, 0)
+        reach = jnp.where(along < broken_at, jnp.exp(log_row), 0.0)
+        q_all[block] = (queries.astype(jnp.float32) * down(reach)).astype(jnp.bfloat16)
+
+    def work(stage):
+        arrays, low, count, slot = stages[stage]
+        each = key_block if len(arrays) > 1 else query_block
+        at_once = max(1, 4 // count)
+
+        def several(step, carry):
+            for extra in range(at_once):
+                for index in range(low, low + count):
+                    each(step * at_once + extra, index)
+            return carry
+
+        lax.fori_loop(0, ctx // at_once, several, 0)
 
     def advance(step, state):
         for extra in range(4):
@@ -198,52 +238,34 @@
             state = gate[block] * state + own[block]
         return state
 
-    lax.fori_loop(0, ctx * blocks // 4, advance, jnp.zeros((BLOCK, BLOCK), jnp.float32))
+    for stage in range(len(stages)):
+        arrived(stage)
+        if stage + AHEAD < len(stages):
+            sent(stage)
+            begin(stage + AHEAD)
+        work(stage)
+        if stage + 1 < len(stages) and len(stages[stage][0]) > len(stages[stage + 1][0]):
+            zero_state = jnp.zeros((BLOCK, BLOCK), jnp.float32)
+            lax.fori_loop(0, total_blocks // 4, advance, zero_state)
 
     ones = jnp.ones((8, BLOCK), jnp.bfloat16)
 
-    def out_copy(bits):
+    def out_copy(bits, arriving):
         there = flipped(me, bits)
-        return pltpu.make_async_remote_copy(
-            src_ref=out_all.at[span(there)],
-            dst_ref=out_hbm.at[:, :, columns(me)],
-            send_sem=out_send.at[bits],
-            recv_sem=out_recv.at[bits],
-            device_id=(there, plane),
-            device_id_type=MESH,
-        )
-
-    def out_landing(bits):
+        origin = there if arriving else me
+        return remote(
+            out_all.at[span(there)],
+            out_hbm.at[:, :, columns(origin)],
+            out_send.at[bits],
+            out_recv.at[bits],
+            there,
+        )
+
+    def sq_copy(bits, arriving):
         there = flipped(me, bits)
-        return pltpu.make_async_remote_copy(
-            src_ref=out_all.at[span(there)],
-            dst_ref=out_hbm.at[:, :, columns(there)],
-            send_sem=out_send.at[bits],
-            recv_sem=out_recv.at[bits],
-            device_id=(there, plane),
-            device_id_type=MESH,
-        )
-
-    def sq_copy(bits):
-        there = flipped(me, bits)
-        return pltpu.make_async_remote_copy(
-            src_ref=squares.at[there],
-            dst_ref=squares_in.at[me],
-            send_sem=sq_send.at[bits],
-            recv_sem=sq_recv.at[bits],
-            device_id=(there, plane),
-            device_id_type=MESH,
-        )
-
-    def sq_landing(bits):
-        there = flipped(me, bits)
-        return pltpu.make_async_remote_copy(
-            src_ref=squares.at[there],
-            dst_ref=squares_in.at[there],
-            send_sem=sq_send.at[bits],
-            recv_sem=sq_recv.at[bits],
-            device_id=(there, plane),
-            device_id_type=MESH,
+        origin = there if arriving else me
+        return remote(
+            squares.at[there], squares_in.at[origin], sq_send.at[bits], sq_recv.at[bits], there
         )
 
     def finish(there):
@@ -260,18 +282,23 @@
 
         lax.fori_loop(0, blocks // 4, several, 0)
 
+    held_back = others[4:]
     for bits in others:
         finish(flipped(me, bits))
-        out_copy(bits).start()
-        sq_copy(bits).start()
+        if bits not in held_back:
+            out_copy(bits, False).start()
+    for bits in others:
+        sq_copy(bits, False).start()
+    for bits in held_back:
+        out_copy(bits, False).start()
     finish(me)
     kept_out = pltpu.make_async_copy(
-        out_all.at[span(me)], out_hbm.at[:, :, columns(me)], out_recv.at[0]
+        out_all.at[span(me)], out_hbm.at[:, :, columns(me)], kept_sem.at[0]
     )
     kept_out.start()
     summed = squares[me]
     for bits in others:
-        sq_landing(bits).wait_recv()
+        sq_copy(bits, True).wait_recv()
         summed = summed + squares_in[flipped(me, bits)]
     share_in[plane] = summed
 
@@ -293,15 +320,15 @@
         share_copy(step, origin).wait_recv()
         total = total + share_in[origin]
     total_ref[...] = total
+    for stage in range(len(stages) - AHEAD, len(stages)):
+        sent(stage)
     kept_out.wait()
     for bits in others:
-        out_landing(bits).wait_recv()
-    for bits in others:
-        log_copy(bits).wait_send()
-        for which in range(ARRAYS):
-            row_copy(bits, which).wait_send()
-        out_copy(bits).wait_send()
-        sq_copy(bits).wait_send()
+        out_copy(bits, True).wait_recv()
+    for bits in others:
+        log_copy(bits, False).wait_send()
+        out_copy(bits, False).wait_send()
+        sq_copy(bits, False).wait_send()
     for step in range(1, head):
         share_copy(step, plane).wait_send()
 
@@ -322,14 +349,6 @@
         log_decay.reshape(blocks, BLOCK, heads),
         preferred_element_type=jnp.float32,
     )
-    starts = jnp.cumsum(doc_lengths) - doc_lengths
-    base = packing * BLOCK
-    relative = starts[None, None, :] - base[:, None, None]
-    begins = jnp.max(jnp.where(relative <= order[None, :, None], relative, -(1 << 24)), axis=2)
-    broken_at = jnp.min(jnp.where(relative >= 0, relative, BLOCK), axis=2)
-    broken_at = jnp.broadcast_to(broken_at, begins.shape)
-    last_begin = jnp.broadcast_to(begins[:, -1:], begins.shape)
-    meta = jnp.stack([begins, broken_at, last_begin], axis=1)
     places = jnp.arange(total_blocks, dtype=jnp.int32)
     source = jnp.sum(
         jnp.where(packing[None, :] == places[:, None], places[None, :], 0), axis=1
@@ -338,6 +357,7 @@
     def in_blocks(values):
         return values.reshape(blocks, BLOCK, width)
 
+    copies = sum(len(stage[0]) for stage in stage_list(blocks))
     any_spec = pl.BlockSpec(memory_space=pl.ANY)
     vmem = pl.BlockSpec(memory_space=pltpu.VMEM)
     dma = pltpu.SemaphoreType.DMA
@@ -347,13 +367,14 @@
             jax.ShapeDtypeStruct((blocks, BLOCK, width), jnp.bfloat16),
             jax.ShapeDtypeStruct((blocks, BLOCK), jnp.float32),
         ),
-        in_specs=[any_spec] * 3 + [vmem, vmem, pl.BlockSpec(memory_space=pltpu.SMEM)],
+        in_specs=[any_spec] * 3 + [vmem] + [pl.BlockSpec(memory_space=pltpu.SMEM)] * 3,
         out_specs=(any_spec, vmem),
         scratch_shapes=[
             pltpu.VMEM((total_blocks, BLOCK, BLOCK), jnp.bfloat16),
             pltpu.VMEM((total_blocks, BLOCK, BLOCK), jnp.bfloat16),
             pltpu.VMEM((total_blocks, BLOCK, BLOCK), jnp.bfloat16),
             pltpu.VMEM((ctx, blocks, BLOCK), jnp.float32),
+            pltpu.VMEM((total_blocks, 8, BLOCK), jnp.int32),
             pltpu.VMEM((total_blocks, BLOCK, BLOCK), jnp.float32),
             pltpu.VMEM((total_blocks, BLOCK, BLOCK), jnp.float32),
             pltpu.VMEM((total_blocks, 1, BLOCK), jnp.float32),
@@ -362,8 +383,9 @@
             pltpu.VMEM((ctx, blocks, BLOCK), jnp.float32),
             pltpu.VMEM((ctx, blocks, BLOCK), jnp.float32),
             pltpu.VMEM((head, blocks, BLOCK), jnp.float32),
-            dma((ctx, ARRAYS)),
-            dma((ctx, ARRAYS)),
+            dma((copies, ctx)),
+            dma((copies, ctx)),
+            dma((ARRAYS + 1,)),
             dma((ctx,)),
             dma((ctx,)),
             dma((ctx,)),
@@ -377,7 +399,7 @@
             collective_id=0, has_side_effects=True, vmem_limit_bytes=52 * 1024 * 1024
         ),
         name="attention_by_head",
-    )(in_blocks(queries), in_blocks(key_rows), in_blocks(value_rows), logs, meta, source)
+    )(in_blocks(queries), in_blocks(key_rows), in_blocks(value_rows), logs, doc_lengths, packing, source)
     scale = lax.rsqrt(squares / (width * head) + 1e-05)
     normed = out.astype(jnp.float32) * scale[:, :, None] * norm_gain[None, None, :]
     return normed.astype(jnp.bfloat16).reshape(rows, width)

time: 213 us -> 209 us (0.981)
  other arithmetic: 7.18 us -> 4.91 us
where the time goes in v2:
time: 209 us; the launch traced here: 207 us
  Pallas kernels  200 us (96%)
  other arithmetic  4.91 us (2%)
  local copies, waits for them, and re-layouts  2.1 us (1%)
    pallas_call x1, Pallas kernels, by_head(): pl.pallas_call(functools.partial(attention_kernel, (ctx, head)), out_shap...  200 us

profile of v2, /device:TPU:4, one launch (start us, length us, event | category | flops | bytes accessed | tf_op | source)
XLA Modules:
  0.0 207.3 jit_solution(13643258196087997097)
XLA Ops:
  0.0 0.0 copy-start
  0.0 0.8 copy-done
  0.8 0.8 select_reduce_fusion.source_ref
  1.5 0.1 convolution_bitcast_fusion.log_ref
  1.7 0.0 copy-start.1
  1.7 0.7 copy-done.1
  2.3 0.0 copy-start.2
  2.4 0.7 copy-done.2
  3.0 0.0 copy-start.3
  3.0 200.1 %attention_by_head.1 = (bf16[16,128,1024]{2,1,0:T(8,128)(2,1)}, f32[16,128]{1,0:T(8,128)S(1)}) custom-call(bf16[16,128,1024]{2,1,0:T(8,128)(2,1)} %bitcast.11, bf16[16,128,1024]{2,1,0:T(8,128)(2,1)} %bitcast.12, bf16[16,128,1024]{2,1,0:T(8,128)(2,1)} %bitcast.13, f32[8,16,128]{2,1,0:T(8,128)S(1)} %convolution_bitcast_fusion.log_ref, s32[16]{0:T(128)S(1)} %copy-done.1, ...), custom_call_target="tpu_custom_call" | custom-call | tf_op jit(solution)/shard_map/attention_by_head/pallas_call | solution.py:364
  203.1 0.0 copy-done.3
  203.1 4.2 %multiply_convert_fusion = bf16[16,128,1024]{2,1,0:T(8,128)(2,1)} fusion(bf16[16,128,1024]{2,1,0:T(8,128)(2,1)} %get-tuple-element.7, f32[1024]{0:T(1024)S(1)} %copy-done.3, f32[16,128]{1,0:T(8,128)S(1)} %add_rsqrt_fusion), kind=kLoop, calls=%fused_computation | loop fusion | flops 8388608 | bytes 8400896 | tf_op jit(solution)/shard_map/convert_element_type | solution.py:405
  (1 shorter events, 0.0 us)
Async XLA Ops:
  0.0 0.8 copy-start
  1.7 0.7 copy-start.1
  2.3 0.7 copy-start.2
  3.0 200.1 %copy-start.3 = (f32[1024]{0:T(1024)S(1)}, f32[1024]{0:T(1024)}, u32[]{:S(2)}) copy-start(f32[1024]{0:T(1024)} %param.11) | copy-start | bytes 12292

commit v3 on v2

--- a/solution.py
+++ b/solution.py
@@ -9,7 +9,7 @@
 
 BLOCK = 128
 MESH = pl.DeviceIdType.MESH
-ORDER = (4, 2, 6, 1, 5, 3, 7)
+ORDER = (4, 2, 5, 3, 6, 7, 1)
 ARRAYS = 3
 AHEAD = 2
 
@@ -31,6 +31,11 @@
     return (
         4 * ((high + bits // 4) % 2) + 2 * ((mid + bits // 2 % 2) % 2) + (low + bits % 2) % 2
     )
+
+
+def turned(me, bits):
+    swapped = 4 * (bits // 2 % 2) + 2 * (bits // 4) + bits % 2
+    return bits + (swapped - bits) * (me % 2)
 
 
 def contract(a, b, dim_a, dim_b):
@@ -134,8 +139,10 @@
             log_ref.at[there], log_all.at[origin], log_send.at[bits], log_recv.at[bits], there
         )
 
+    sequence = [turned(me, bits) for bits in others]
+
     def begin(stage):
-        for bits in others:
+        for bits in sequence:
             for copy in row_copies(stage, bits, False):
                 copy.start()
 
@@ -282,14 +289,13 @@
 
         lax.fori_loop(0, blocks // 4, several, 0)
 
-    held_back = others[4:]
-    for bits in others:
+    for index, bits in enumerate(sequence):
         finish(flipped(me, bits))
-        if bits not in held_back:
+        if index < 4:
             out_copy(bits, False).start()
     for bits in others:
         sq_copy(bits, False).start()
-    for bits in held_back:
+    for bits in sequence[4:]:
         out_copy(bits, False).start()
     finish(me)
     kept_out = pltpu.make_async_copy(

time: 209 us -> 210 us (level)
  no operation moved by 1% of the time
where the time goes in v3:
time: 210 us; the launch traced here: 208 us
  Pallas kernels  201 us (96%)
  other arithmetic  4.91 us (2%)
  local copies, waits for them, and re-layouts  2.1 us (1%)
    pallas_call x1, Pallas kernels, by_head(): pl.pallas_call(functools.partial(attention_kernel, (ctx, head)), out_shap...  201 us

profile of v3, /device:TPU:4, one launch (start us, length us, event | category | flops | bytes accessed | tf_op | source)
XLA Modules:
  0.0 207.8 jit_solution(15662935839934771492)
XLA Ops:
  0.0 0.0 copy-start
  0.0 0.8 copy-done
  0.8 0.8 select_reduce_fusion.source_ref
  1.5 0.1 convolution_bitcast_fusion.log_ref
  1.7 0.0 copy-start.1
  1.7 0.7 copy-done.1
  2.3 0.0 copy-start.2
  2.4 0.7 copy-done.2
  3.0 0.0 copy-start.3
  3.0 200.6 %attention_by_head.1 = (bf16[16,128,1024]{2,1,0:T(8,128)(2,1)}, f32[16,128]{1,0:T(8,128)S(1)}) custom-call(bf16[16,128,1024]{2,1,0:T(8,128)(2,1)} %bitcast.11, bf16[16,128,1024]{2,1,0:T(8,128)(2,1)} %bitcast.12, bf16[16,128,1024]{2,1,0:T(8,128)(2,1)} %bitcast.13, f32[8,16,128]{2,1,0:T(8,128)S(1)} %convolution_bitcast_fusion.log_ref, s32[16]{0:T(128)S(1)} %copy-done.1, ...), custom_call_target="tpu_custom_call" | custom-call | tf_op jit(solution)/shard_map/attention_by_head/pallas_call | solution.py:370
  203.7 0.0 copy-done.3
  203.7 4.2 %multiply_convert_fusion = bf16[16,128,1024]{2,1,0:T(8,128)(2,1)} fusion(bf16[16,128,1024]{2,1,0:T(8,128)(2,1)} %get-tuple-element.7, f32[1024]{0:T(1024)S(1)} %copy-done.3, f32[16,128]{1,0:T(8,128)S(1)} %add_rsqrt_fusion), kind=kLoop, calls=%fused_computation | loop fusion | flops 8388608 | bytes 8400896 | tf_op jit(solution)/shard_map/convert_element_type | solution.py:411
  (1 shorter events, 0.0 us)
Async XLA Ops:
  0.0 0.8 copy-start
  1.7 0.7 copy-start.1
  2.3 0.7 copy-start.2
  3.0 200.7 %copy-start.3 = (f32[1024]{0:T(1024)S(1)}, f32[1024]{0:T(1024)}, u32[]{:S(2)}) copy-start(f32[1024]{0:T(1024)} %param.11) | copy-start | bytes 12292

commit v4 on v3

--- a/solution.py
+++ b/solution.py
@@ -68,6 +68,10 @@
     squares,
     squares_in,
     share_in,
+    k_held,
+    v_held,
+    q_held,
+    held_sem,
     send_sem,
     recv_sem,
     kept_sem,
@@ -87,6 +91,23 @@
     total_blocks = ctx * blocks
     others = ORDER
 
+    def columns(index):
+        return pl.ds(pl.multiple_of(index * BLOCK, BLOCK), BLOCK)
+
+    held = ((k_hbm, k_held), (v_hbm, v_held), (q_hbm, q_held))
+
+    def hold(which, bits):
+        there = flipped(me, bits)
+        return pltpu.make_async_copy(
+            held[which][0].at[:, :, columns(there)],
+            held[which][1].at[pl.ds(there * blocks, blocks)],
+            held_sem.at[which, bits],
+        )
+
+    for which in range(ARRAYS):
+        for bits in others:
+            hold(which, bits).start()
+
     barrier = pltpu.get_barrier_semaphore()
     for bits in others:
         pl.semaphore_signal(
@@ -100,9 +121,6 @@
 
     pairs = ((k_hbm, k_all), (v_hbm, v_all), (q_hbm, q_all))
     stages = stage_list(blocks)
-
-    def columns(index):
-        return pl.ds(pl.multiple_of(index * BLOCK, BLOCK), BLOCK)
 
     def span(index, low=0, count=blocks):
         return pl.ds(index * blocks + low, count)
@@ -123,7 +141,7 @@
         origin = there if arriving else me
         return [
             remote(
-                pairs[which][0].at[pl.ds(low, count), :, columns(there)],
+                held[which][1].at[span(there, low, count)],
                 pairs[which][1].at[span(origin, low, count)],
                 send_sem.at[slot + extra, bits],
                 recv_sem.at[slot + extra, bits],
@@ -158,8 +176,13 @@
 
     for bits in others:
         log_copy(bits, False).start()
+    for which in range(2):
+        for bits in others:
+            hold(which, bits).wait()
     for stage in range(AHEAD):
         begin(stage)
+    for bits in others:
+        hold(2, bits).wait()
     kept = [
         pltpu.make_async_copy(
             source.at[:, :, columns(me)], landing.at[span(me)], kept_sem.at[index]
@@ -262,7 +285,7 @@
         origin = there if arriving else me
         return remote(
             out_all.at[span(there)],
-            out_hbm.at[:, :, columns(origin)],
+            out_hbm.at[origin],
             out_send.at[bits],
             out_recv.at[bits],
             there,
@@ -299,7 +322,7 @@
         out_copy(bits, False).start()
     finish(me)
     kept_out = pltpu.make_async_copy(
-        out_all.at[span(me)], out_hbm.at[:, :, columns(me)], kept_sem.at[0]
+        out_all.at[span(me)], out_hbm.at[me], kept_sem.at[0]
     )
     kept_out.start()
     summed = squares[me]
@@ -339,6 +362,15 @@
         share_copy(step, plane).wait_send()
 
 
+def norm_kernel(count, out_ref, squares_ref, gain_ref, mixed_ref):
+    scale = lax.rsqrt(squares_ref[0] / count + 1e-05)
+    down = jnp.transpose(jnp.broadcast_to(scale, (BLOCK, BLOCK)))
+    for index in range(out_ref.shape[0]):
+        at = slice(index * BLOCK, (index + 1) * BLOCK)
+        values = out_ref[index, 0].astype(jnp.float32) * down * gain_ref[:, at]
+        mixed_ref[:, at] = values.astype(jnp.bfloat16)
+
+
 def by_head(queries, key_rows, value_rows, log_decay, norm_gain, doc_lengths, packing):
     rows, width = queries.shape
     heads = log_decay.shape[1]
@@ -370,7 +402,7 @@
     out, squares = pl.pallas_call(
         functools.partial(attention_kernel, (ctx, head)),
         out_shape=(
-            jax.ShapeDtypeStruct((blocks, BLOCK, width), jnp.bfloat16),
+            jax.ShapeDtypeStruct((ctx, blocks, BLOCK, BLOCK), jnp.bfloat16),
             jax.ShapeDtypeStruct((blocks, BLOCK), jnp.float32),
         ),
         in_specs=[any_spec] * 3 + [vmem] + [pl.BlockSpec(memory_space=pltpu.SMEM)] * 3,
@@ -389,6 +421,10 @@
             pltpu.VMEM((ctx, blocks, BLOCK), jnp.float32),
             pltpu.VMEM((ctx, blocks, BLOCK), jnp.float32),
             pltpu.VMEM((head, blocks, BLOCK), jnp.float32),
+            pltpu.VMEM((total_blocks, BLOCK, BLOCK), jnp.bfloat16),
+            pltpu.VMEM((total_blocks, BLOCK, BLOCK), jnp.bfloat16),
+            pltpu.VMEM((total_blocks, BLOCK, BLOCK), jnp.bfloat16),
+            dma((ARRAYS, ctx)),
             dma((copies, ctx)),
             dma((copies, ctx)),
             dma((ARRAYS + 1,)),
@@ -402,13 +438,22 @@
             dma((head,)),
         ],
         compiler_params=pltpu.CompilerParams(
-            collective_id=0, has_side_effects=True, vmem_limit_bytes=52 * 1024 * 1024
+            collective_id=0, has_side_effects=True, vmem_limit_bytes=58 * 1024 * 1024
         ),
         name="attention_by_head",
     )(in_blocks(queries), in_blocks(key_rows), in_blocks(value_rows), logs, doc_lengths, packing, source)
-    scale = lax.rsqrt(squares / (width * head) + 1e-05)
-    normed = out.astype(jnp.float32) * scale[:, :, None] * norm_gain[None, None, :]
-    return normed.astype(jnp.bfloat16).reshape(rows, width)
+    return pl.pallas_call(
+        functools.partial(norm_kernel, width * head),
+        grid=(blocks,),
+        out_shape=jax.ShapeDtypeStruct((rows, width), jnp.bfloat16),
+        in_specs=[
+            pl.BlockSpec((ctx, 1, BLOCK, BLOCK), lambda n: (0, n, 0, 0)),
+            pl.BlockSpec((1, 1, BLOCK), lambda n: (n, 0, 0)),
+            pl.BlockSpec((1, width), lambda n: (0, 0)),
+        ],
+        out_specs=pl.BlockSpec((BLOCK, width), lambda n: (n, 0)),
+        name="norm_rows",
+    )(out, squares.reshape(blocks, 1, BLOCK), norm_gain.reshape(1, width))
 
 
 def from_behind(x, axis, by):

time: 210 us -> 219 us (1.043)
  Pallas kernels: 201 us -> 215 us
  other arithmetic: 4.91 us -> 1.31 us
    pallas_call x0 -> x1, Pallas kernels: none -> 11 us  [by_head(): pl.pallas_call(functools.partial(norm_kernel, width * head), grid=(blocks...]
    convert_element_type x1 -> x0, other arithmetic: 4.15 us -> none  [by_head(): return normed.astype(jnp.bfloat16).reshape(rows, width)]
    pallas_call x1, Pallas kernels: 201 us -> 204 us  [by_head(): pl.pallas_call(functools.partial(attention_kernel, (ctx, head)), out_shap...]
where the time goes in v4:
time: 219 us; the launch traced here: 218 us
  Pallas kernels  215 us (98%)
    pallas_call x1, Pallas kernels, by_head(): pl.pallas_call(functools.partial(attention_kernel, (ctx, head)), out_shap...  204 us
    pallas_call x1, Pallas kernels, by_head(): pl.pallas_call(functools.partial(norm_kernel, width * head), grid=(blocks...  11 us

profile of v4, /device:TPU:4, one launch (start us, length us, event | category | flops | bytes accessed | tf_op | source)
XLA Modules:
  0.0 218.1 jit_solution(15468778496030595887)
XLA Ops:
  0.0 0.0 copy-start
  0.0 0.8 copy-done
  0.8 1.3 select_reduce_fusion.source_ref
  2.1 0.8 convolution_bitcast_fusion.log_ref
  2.9 204.3 %attention_by_head.1 = (bf16[8,16,128,128]{3,2,1,0:T(8,128)(2,1)}, f32[16,128]{1,0:T(8,128)}) custom-call(bf16[16,128,1024]{2,1,0:T(8,128)(2,1)} %bitcast.12, bf16[16,128,1024]{2,1,0:T(8,128)(2,1)} %bitcast.13, bf16[16,128,1024]{2,1,0:T(8,128)(2,1)} %bitcast.14, f32[8,16,128]{2,1,0:T(8,128)} %convolution_bitcast_fusion.log_ref, s32[16]{0:T(128)} %length_ref.1, ...), custom_call_target="tpu_custom_call" | custom-call | tf_op jit(solution)/shard_map/attention_by_head/pallas_call | solution.py:402
  207.1 11.0 %norm_rows.1 = bf16[2048,1024]{1,0:T(8,128)(2,1)} custom-call(bf16[8,16,128,128]{3,2,1,0:T(8,128)(2,1)} %get-tuple-element.7.out_ref, f32[16,1,128]{2,1,0:T(1,128)} %bitcast.15, f32[1,1024]{1,0:T(1,128)} %bitcast.16), custom_call_target="tpu_custom_call" | custom-call | tf_op jit(solution)/shard_map/norm_rows/pallas_call | solution.py:445
Async XLA Ops:
  0.0 0.8 copy-start

commit v5 on v3

--- a/solution.py
+++ b/solution.py
@@ -60,6 +60,7 @@
     v_all,
     log_all,
     meta,
+    q_decayed,
     intra,
     own,
     gate,
@@ -200,39 +201,66 @@
     def down(row):
         return jnp.transpose(jnp.broadcast_to(row, (BLOCK, BLOCK)))
 
-    def key_block(there, index):
-        block = there * blocks + index
-        log_row = log_all[there, index : index + 1, :]
-        last_begin = meta[block, 2:3, :]
-        total = jnp.broadcast_to(log_row[:, BLOCK - 1 :], (1, BLOCK))
-        keep = jnp.where(along >= last_begin, jnp.exp(total - log_row), 0.0)
-        decayed = (k_all[block].astype(jnp.float32) * down(keep)).astype(jnp.bfloat16)
-        own[block] = contract(decayed, v_all[block], 0, 0)
-        gate[block] = jnp.where(last_begin < 0, jnp.exp(total), 0.0)
-
-    def query_block(there, index):
-        block = there * blocks + index
-        log_row = log_all[there, index : index + 1, :]
-        begins = meta[block, 0:1, :]
-        broken_at = meta[block, 1:2, :]
-        queries = q_all[block]
-        scores = contract(k_all[block], queries, 1, 1)
-        allowed = (sub >= begins) & (sub <= lane)
-        gaps = jnp.minimum(log_row - down(log_row), 0.0)
-        weights = jnp.where(allowed, scores * jnp.exp(gaps), 0.0).astype(jnp.bfloat16)
-        intra[block] = contract(weights, v_all[block], 0, 0)
-        reach = jnp.where(along < broken_at, jnp.exp(log_row), 0.0)
-        q_all[block] = (queries.astype(jnp.float32) * down(reach)).astype(jnp.bfloat16)
+    def key_blocks(places):
+        rows = [log_all[there, index : index + 1, :] for there, index in places]
+        ids = [there * blocks + index for there, index in places]
+        marks = [meta[block, 2:3, :] for block in ids]
+        keys = [k_all[block] for block in ids]
+        values = [v_all[block] for block in ids]
+        totals = [jnp.broadcast_to(row[:, BLOCK - 1 :], (1, BLOCK)) for row in rows]
+        keeps = [
+            down(jnp.where(along >= begin_at, jnp.exp(total - row), 0.0))
+            for row, total, begin_at in zip(rows, totals, marks)
+        ]
+        decayed = [
+            (key.astype(jnp.float32) * keep).astype(jnp.bfloat16)
+            for key, keep in zip(keys, keeps)
+        ]
+        results = [contract(key, value, 0, 0) for key, value in zip(decayed, values)]
+        for block, result, total, begin_at in zip(ids, results, totals, marks):
+            own[block] = result
+            gate[block] = jnp.where(begin_at < 0, jnp.exp(total), 0.0)
+
+    def query_blocks(places):
+        rows = [log_all[there, index : index + 1, :] for there, index in places]
+        ids = [there * blocks + index for there, index in places]
+        begins = [meta[block, 0:1, :] for block in ids]
+        broken = [meta[block, 1:2, :] for block in ids]
+        queries = [q_all[block] for block in ids]
+        keys = [k_all[block] for block in ids]
+        values = [v_all[block] for block in ids]
+        scores = [contract(key, query, 1, 1) for key, query in zip(keys, queries)]
+        downs = [down(row) for row in rows]
+        reaches = [
+            down(jnp.where(along < stop, jnp.exp(row), 0.0)) for row, stop in zip(rows, broken)
+        ]
+        weights = []
+        for row, column, begin_at, score in zip(rows, downs, begins, scores):
+            allowed = (sub >= begin_at) & (sub <= lane)
+            factor = jnp.exp(jnp.minimum(row - column, 0.0))
+            weights.append(jnp.where(allowed, score * factor, 0.0).astype(jnp.bfloat16))
+        results = [contract(weight, value, 0, 0) for weight, value in zip(weights, values)]
+        decayed = [
+            (query.astype(jnp.float32) * reach).astype(jnp.bfloat16)
+            for query, reach in zip(queries, reaches)
+        ]
+        for block, result, query in zip(ids, results, decayed):
+            intra[block] = result
+            q_decayed[block] = query
 
     def work(stage):
         arrays, low, count, slot = stages[stage]
-        each = key_block if len(arrays) > 1 else query_block
+        each = key_blocks if len(arrays) > 1 else query_blocks
         at_once = max(1, 4 // count)
 
         def several(step, carry):
-            for extra in range(at_once):
-                for index in range(low, low + count):
-                    each(step * at_once + extra, index)
+            each(
+                [
+                    (step * at_once + extra, index)
+                    for extra in range(at_once)
+                    for index in range(low, low + count)
+                ]
+            )
             return carry
 
         lax.fori_loop(0, ctx // at_once, several, 0)
@@ -277,14 +305,20 @@
 
     def finish(there):
         def several(step, carry):
-            for extra in range(4):
-                index = step * 4 + extra
-                place = there * blocks + index
-                block = source_ref[place]
-                result = intra[block] + contract(q_all[block], states[place], 1, 0)
+            indices = [step * 4 + extra for extra in range(4)]
+            places = [there * blocks + index for index in indices]
+            ids = [source_ref[place] for place in places]
+            terms = [intra[block] for block in ids]
+            products = [
+                contract(q_decayed[block], states[place], 1, 0) for block, place in zip(ids, places)
+            ]
+            results = [term + product for term, product in zip(terms, products)]
+            summed = [
+                contract(ones, (result * result).astype(jnp.bfloat16), 1, 1) for result in results
+            ]
+            for index, place, result, line in zip(indices, places, results, summed):
                 out_all[place] = result.astype(jnp.bfloat16)
-                summed = contract(ones, (result * result).astype(jnp.bfloat16), 1, 1)
-                squares[there, pl.ds(index, 1), :] = summed[0:1]
+                squares[there, pl.ds(index, 1), :] = line[0:1]
             return carry
 
         lax.fori_loop(0, blocks // 4, several, 0)
@@ -381,6 +415,7 @@
             pltpu.VMEM((total_blocks, BLOCK, BLOCK), jnp.bfloat16),
             pltpu.VMEM((ctx, blocks, BLOCK), jnp.float32),
             pltpu.VMEM((total_blocks, 8, BLOCK), jnp.int32),
+            pltpu.VMEM((total_blocks, BLOCK, BLOCK), jnp.bfloat16),
             pltpu.VMEM((total_blocks, BLOCK, BLOCK), jnp.float32),
             pltpu.VMEM((total_blocks, BLOCK, BLOCK), jnp.float32),
             pltpu.VMEM((total_blocks, 1, BLOCK), jnp.float32),

time: 210 us -> 207 us (0.986)
  Pallas kernels: 201 us -> 198 us
    pallas_call x1, Pallas kernels: 201 us -> 198 us  [by_head(): pl.pallas_call(functools.partial(attention_kernel, (ctx, head)), out_shap...]
where the time goes in v5:
time: 207 us; the launch traced here: 205 us
  Pallas kernels  198 us (96%)
  other arithmetic  4.91 us (2%)
  local copies, waits for them, and re-layouts  2.1 us (1%)
    pallas_call x1, Pallas kernels, by_head(): pl.pallas_call(functools.partial(attention_kernel, (ctx, head)), out_shap...  198 us
    convert_element_type x1, other arithmetic, by_head(): return normed.astype(jnp.bfloat16).reshape(rows, width)  4.15 us

profile of v5, /device:TPU:4, one launch (start us, length us, event | category | flops | bytes accessed | tf_op | source)
XLA Modules:
  0.0 205.0 jit_solution(5016478018529501050)
XLA Ops:
  0.0 0.0 copy-start
  0.0 0.8 copy-done
  0.8 0.8 select_reduce_fusion.source_ref
  1.5 0.1 convolution_bitcast_fusion.log_ref
  1.7 0.0 copy-start.1
  1.7 0.7 copy-done.1
  2.3 0.0 copy-start.2
  2.4 0.7 copy-done.2
  3.0 0.0 copy-start.3
  3.0 197.9 %attention_by_head.1 = (bf16[16,128,1024]{2,1,0:T(8,128)(2,1)}, f32[16,128]{1,0:T(8,128)S(1)}) custom-call(bf16[16,128,1024]{2,1,0:T(8,128)(2,1)} %bitcast.11, bf16[16,128,1024]{2,1,0:T(8,128)(2,1)} %bitcast.12, bf16[16,128,1024]{2,1,0:T(8,128)(2,1)} %bitcast.13, f32[8,16,128]{2,1,0:T(8,128)S(1)} %convolution_bitcast_fusion.log_ref, s32[16]{0:T(128)S(1)} %copy-done.1, ...), custom_call_target="tpu_custom_call" | custom-call | tf_op jit(solution)/shard_map/attention_by_head/pallas_call | solution.py:404
  200.9 0.0 copy-done.3
  200.9 4.2 %multiply_convert_fusion = bf16[16,128,1024]{2,1,0:T(8,128)(2,1)} fusion(bf16[16,128,1024]{2,1,0:T(8,128)(2,1)} %get-tuple-element.7, f32[1024]{0:T(1024)S(1)} %copy-done.3, f32[16,128]{1,0:T(8,128)S(1)} %add_rsqrt_fusion), kind=kLoop, calls=%fused_computation | loop fusion | flops 8388608 | bytes 8400896 | tf_op jit(solution)/shard_map/convert_element_type | solution.py:446
  (1 shorter events, 0.0 us)
Async XLA Ops:
  0.0 0.8 copy-start
  1.7 0.7 copy-start.1
  2.3 0.7 copy-start.2
  3.0 197.9 %copy-start.3 = (f32[1024]{0:T(1024)S(1)}, f32[1024]{0:T(1024)}, u32[]{:S(2)}) copy-start(f32[1024]{0:T(1024)} %param.11) | copy-start | bytes 12292
